TPU v7x, 1024 devices: a whole 4x4x32 slice. The times are simulated.
1024 devices in a mesh: group: 16 (over y, x), cuts: 64 (over z, core).
Axes of the slice: x: 4, y: 4, z: 32, core: 2. Of those that a mesh axis runs over, the one named last changes fastest.
Arguments:
- gradient: float32 [3, 16, 2048, 128], P(None, 'group', 'cuts'), may hold values from -6 to 6
- basis: bfloat16 [16, 2048, 128, 128], P('group', 'cuts'), may hold values from -0.5 to 0.5
- block_owner: int32 [16, 2048, 1], P('group', 'cuts'), may hold values from 0 to 63; in each aligned block of 32 rows (0 to 31, 32 to 63, ..., all dimensions but the last counted through in order) at most 2 rows name the same one
- block_local: int32 [16, 2048], P('group', 'cuts'), may hold values from 0 to 15
- valid_count: int32 [16, 2048], P('group', 'cuts'), may hold values from 32 to 128
- band_offsets: int32 [4], replicated, may hold values from -16 to 16
- band_weight: float32 [3, 4], replicated, may hold values from 0.02 to 0.12
- radial_weight: float32 [3], replicated, may hold values from 0.05 to 0.2
Outputs:
- smoothed_gradient: float32 [3, 16, 2048, 128], P(None, 'group', 'cuts')
Inputs may be any that keep to these rules, and one draw needn't show every extreme that they name: `block_owner`: among the blocks of one device, at most 2 have the same owner, a bound that some of them reach.
All inputs are finite; a program needn't handle non-finite values.
Results may differ from a plain program's by a relative error of at most 0.0038.
Values may be sent and summed in bfloat16 or wider, within the bound.
No kernel may reach another device: no remote copies, remote signals or barrier semaphores. Data moves between devices by JAX's collectives and lax.ppermute only.
A program may use at most 32 MiB of HBM per device.

v0:
```python
import jax
import jax.numpy as jnp
from jax import lax
from jax.sharding import PartitionSpec as P

PD = 16
BANDS = 4


def extended(value, sides, width, wrap):
    for axis, dim in sides:
        size, length = (lax.axis_size(axis), value.shape[dim])
        up = [(i, (i + 1) % size) for i in range(size if wrap else size - 1)]
        down = [(j, i) for i, j in up]
        last = lax.slice_in_dim(value, length - width, length, axis=dim)
        first = lax.slice_in_dim(value, 0, width, axis=dim)
        before = lax.ppermute(last, axis, up)
        after = lax.ppermute(first, axis, down)
        value = jnp.concatenate([before, value, after], axis=dim)
    return value


def body(
    gradient, basis, block_owner, block_local, valid_count, band_offsets, band_weight, radial_weight
):
    params = gradient.shape[0]
    blocks = gradient.shape[2]
    points_per = gradient.shape[3]
    width = basis.shape[3]
    patches = PD
    points = jnp.arange(points_per, dtype=jnp.int32)
    inside = points[None, :] < valid_count[0][:, None]
    masked_values = jnp.where(inside[None], gradient[:, 0], 0.0).astype(jnp.bfloat16)
    projected_gradient = jnp.einsum(
        "xrg,rgv->rxv", masked_values, basis[0], preferred_element_type=jnp.float32
    )
    projected_gradient = projected_gradient.reshape(blocks, params * width)
    owner_index = block_owner[0, :, 0]
    local_patch = block_local[0]
    patch_index = owner_index * patches + local_patch
    wanted = jnp.arange(patches * lax.axis_size("cuts"), dtype=jnp.int32)
    onehot = (patch_index[:, None] == wanted[None, :]).astype(jnp.float32)
    coefficients = lax.psum_scatter(
        jnp.dot(onehot.T, projected_gradient, precision=lax.Precision.HIGHEST),
        "cuts",
        scatter_dimension=0,
        tiled=True,
    )
    stacked = coefficients[None]
    lateral = extended(stacked, (("cuts", 1),), patches, True)[0]
    radial = extended(stacked, (("group", 0),), 1, False)
    lateral_sum = jnp.zeros_like(coefficients)
    for band_number_index in range(BANDS):
        shifted = lax.dynamic_slice_in_dim(
            lateral, patches + band_offsets[band_number_index], patches, 0
        )
        band_column = jnp.repeat(band_weight[:, band_number_index], width)
        lateral_sum = lateral_sum + band_column[None, :] * (shifted - coefficients)
    radial_depth_column = jnp.repeat(radial_weight, width)
    radial_sum = radial_depth_column[None, :] * (radial[0] + radial[2] - 2.0 * coefficients)
    smooth = (coefficients + lateral_sum + radial_sum).astype(jnp.bfloat16)
    gathered = lax.all_gather(smooth, "cuts", axis=0, tiled=True)
    picked_rows = jnp.take(gathered, patch_index, axis=0)
    picked_rows = picked_rows.reshape(blocks, params, width)
    broadcast_values = jnp.einsum(
        "xfh,xah->axf", basis[0], picked_rows, preferred_element_type=jnp.float32
    )
    broadcast_values = jnp.where(inside[None], broadcast_values, 0.0)
    return broadcast_values[:, None]


def solution(mesh):
    return jax.shard_map(
        body,
        mesh=mesh,
        in_specs=(
            P(None, "group", "cuts", None),
            P("group", "cuts", None, None),
            P("group", "cuts", None),
            P("group", "cuts"),
            P("group", "cuts"),
            P(),
            P(),
            P(),
        ),
        out_specs=P(None, "group", "cuts", None),
        check_vma=False,
    )
```

profile of v0, /device:TPU:24, one launch (start us, length us, event | category | flops | bytes accessed | tf_op | source)
XLA Modules:
  0.0 311.4 jit_solution(17528441465372973971)
XLA Ops:
  6.5 0.0 copy-start
  6.5 0.0 reduce-scatter.2.cloned.1.call-start
  6.5 0.8 iota_compare_fusion.2
  7.4 0.8 fusion.8
  8.2 0.0 copy-done
  8.2 0.4 fusion.2
  8.5 0.7 compare_and_fusion
  9.2 0.0 copy-start.2
  9.2 0.0 copy-start.1
  9.2 0.0 copy-start.4
  9.3 0.0 copy-start.5
  9.3 0.0 copy-start.3
  9.3 2.1 fusion.4
  11.3 0.0 reduce-scatter.2.cloned.1.call-update
  11.4 0.0 copy-done.2
  11.4 0.7 fusion.26
  12.0 0.0 copy-done.1
  12.0 0.2 slice_reduce_fusion.3
  12.2 0.0 copy-done.4
  12.3 0.0 copy-done.5
  12.3 0.0 copy-done.3
  12.3 0.1 broadcast_bitcast_fusion
  12.4 0.1 broadcast_bitcast_fusion.1
  12.4 0.1 broadcast_bitcast_fusion.3
  12.5 216.7 %reduce-scatter.2.cloned.1.call-done = f32[16,384]{1,0:T(8,128)} async-done(((f32[1024,384]{1,0:T(8,128)}), f32[16,384]{1,0:T(8,128)}) %reduce-scatter.2.cloned.1.call-update) | async-done | bytes 24592 | tf_op jit(solution)/shard_map/reduce_scatter | solution.py:43
  229.2 0.0 collective-permute-start
  229.2 3.0 collective-permute-start.1
  237.3 3.4 %collective-permute-start.2 = (f32[1,16,384]{2,1,0:T(8,128)}, f32[1,16,384]{2,1,0:T(8,128)S(1)}, u32[]{:S(2)}, u32[]{:S(2)}) collective-permute-start(f32[1,16,384]{2,1,0:T(8,128)} %bitcast.94), channel_id=1, source_target_pairs={{0,64},{64,128},{128,192},{192,256},{256,320},{320,384},{384,448},... | collective-permute-start | bytes 73736 | tf_op jit(solution)/shard_map/ppermute | solution.py:17
  240.6 4.6 %collective-permute-start.3 = (f32[1,16,384]{2,1,0:T(8,128)}, f32[1,16,384]{2,1,0:T(8,128)S(1)}, u32[]{:S(2)}, u32[]{:S(2)}) collective-permute-start(f32[1,16,384]{2,1,0:T(8,128)} %bitcast.95), channel_id=1, source_target_pairs={{64,0},{128,64},{192,128},{256,192},{320,256},{384,320},{448,384},... | collective-permute-start | bytes 73736 | tf_op jit(solution)/shard_map/ppermute | solution.py:18
  245.2 0.0 collective-permute-done
  245.2 0.0 collective-permute-done.1
  245.3 0.8 pad_maximum_fusion
  246.0 0.0 collective-permute-done.2
  246.0 0.9 collective-permute-done.3
  246.9 0.8 fusion.14
  247.7 54.9 %all_gather.3 = bf16[1024,384]{1,0:T(8,128)(2,1)S(1)} all-gather(bf16[16,384]{1,0:T(8,128)(2,1)S(1)} %fusion.14), channel_id=1, replica_groups=mesh['group'=16,'cuts'=64] {'cuts'}, dimensions={0}, use_global_device_ids=true | all-gather | bytes 798720 | tf_op jit(solution)/shard_map/all_gather | solution.py:62
  302.6 0.6 gather_fusion
  303.2 0.7 fusion
  303.9 0.6 copy.12
  (3 shorter events, 0.0 us)
Async XLA Ops:
  6.5 1.6 copy-start
  6.5 222.7 %reduce-scatter.2.cloned.1.call-start = ((), (), s32[]{:S(2)}) async-start(), calls=%async_computation.1 | async-start | bytes 1597440 | tf_op jit(solution)/shard_map/reduce_scatter | solution.py:43
  9.2 2.1 copy-start.2
  9.2 2.8 copy-start.1
  9.2 3.0 copy-start.4
  9.3 3.0 copy-start.5
  9.3 3.0 copy-start.3
  229.2 16.0 %collective-permute-start = (f32[1,16,384]{2,1,0:T(8,128)}, f32[1,16,384]{2,1,0:T(8,128)S(1)}, u32[]{:S(2)}, u32[]{:S(2)}) collective-permute-start(f32[1,16,384]{2,1,0:T(8,128)} %bitcast.92), channel_id=1, source_target_pairs={{0,1},{1,2},{2,3},{3,4},{4,5},{5,6},{6,7},{7,8},{8,9},{9,10},{10,1... | collective-permute-start | bytes 73736 | tf_op jit(solution)/shard_map/ppermute | solution.py:17
  229.2 16.0 %collective-permute-start.1 = (f32[1,16,384]{2,1,0:T(8,128)}, f32[1,16,384]{2,1,0:T(8,128)S(1)}, u32[]{:S(2)}, u32[]{:S(2)}) collective-permute-start(f32[1,16,384]{2,1,0:T(8,128)} %bitcast.93), channel_id=1, source_target_pairs={{1,0},{2,1},{3,2},{4,3},{5,4},{6,5},{7,6},{8,7},{9,8},{10,9},{11,1... | collective-permute-start | bytes 73736 | tf_op jit(solution)/shard_map/ppermute | solution.py:18
  237.3 8.8 %collective-permute-start.2 = (f32[1,16,384]{2,1,0:T(8,128)}, f32[1,16,384]{2,1,0:T(8,128)S(1)}, u32[]{:S(2)}, u32[]{:S(2)}) collective-permute-start(f32[1,16,384]{2,1,0:T(8,128)} %bitcast.94), channel_id=1, source_target_pairs={{0,64},{64,128},{128,192},{192,256},{256,320},{320,384},{384,448},... | collective-permute-start | bytes 73736 | tf_op jit(solution)/shard_map/ppermute | solution.py:17
  240.6 6.3 %collective-permute-start.3 = (f32[1,16,384]{2,1,0:T(8,128)}, f32[1,16,384]{2,1,0:T(8,128)S(1)}, u32[]{:S(2)}, u32[]{:S(2)}) collective-permute-start(f32[1,16,384]{2,1,0:T(8,128)} %bitcast.95), channel_id=1, source_target_pairs={{64,0},{128,64},{192,128},{256,192},{320,256},{384,320},{448,384},... | collective-permute-start | bytes 73736 | tf_op jit(solution)/shard_map/ppermute | solution.py:18
Sparse Core Ops, SparseCore 0:
  11.5 217.6 reduce-scatter.1
where the time goes:
time: 315 us; the launch traced here: 311 us
  waiting for transfers between devices  218 us (69%)
  blocking collectives  54.9 us (17%)
  between operations  18.6 us (6%)
  starting transfers between devices  10.9 us (3%)
  other arithmetic  3.86 us (1%)
    reduce_scatter x1, waiting for transfers between devices, body(): lax.psum_scatter(jnp.dot(onehot.T, projected_gradient, precision=lax.Prec...  217 us
    all_gather x1, blocking collectives, body(): gathered = lax.all_gather(smooth, 'cuts', axis=0, tiled=True)  54.9 us
    ppermute x2, starting transfers between devices, extended(): after = lax.ppermute(first, axis, down)  7.54 us
  transfers between devices with their start and end apart: 5, of which 2 were waited for; matrix products, arithmetic and copies ran while one was open for 1% of the time, Pallas kernels for 0%

commit v1 on v0

v1 whole, which is shorter than its diff:
```python
import jax
import jax.numpy as jnp
from jax import lax
from jax.experimental import pallas as pl
from jax.experimental.pallas import tpu as pltpu
from jax.sharding import PartitionSpec as P

PD = 16
CORES = 2
ID_ROWS = 8


def column(row, count):
    lanes = row.shape[1]
    wide = jnp.broadcast_to(row, (count, lanes))
    at = lax.broadcasted_iota(jnp.int32, (count, lanes), 0) == lax.broadcasted_iota(
        jnp.int32, (count, lanes), 1
    )
    return jnp.sum(jnp.where(at, wide, 0), axis=1, keepdims=True)


def inside_mask(valid_ref, blocks, points):
    count = column(valid_ref[...], blocks)
    return lax.broadcasted_iota(jnp.int32, (blocks, points), 1) < count


def project_kernel(
    gradient_hbm, basis_hbm, patch_ref, valid_ref, payload_ref, gradient_ref, basis_ref, rows_ref, ids_ref, done
):
    copies = [
        pltpu.make_async_copy(gradient_hbm, gradient_ref, done.at[0]),
        pltpu.make_async_copy(basis_hbm, basis_ref, done.at[1]),
    ]
    for copy in copies:
        copy.start()
    params, _, blocks, points = gradient_ref.shape
    inside = inside_mask(valid_ref, blocks, points)
    ids_ref[...] = jnp.zeros_like(ids_ref)
    ids_ref[0:1, 0:blocks] = patch_ref[...] // PD
    ids_ref[1:2, 0:blocks] = patch_ref[...] % PD
    position = lax.axis_index("cuts")
    quarter = (position // (2 * CORES)) % 2 * CORES + position % CORES
    ids = pltpu.roll(ids_ref[...].astype(jnp.float32), quarter * blocks, 1)
    payload_ref[params * blocks :, :] = ids.astype(jnp.bfloat16)
    copies[0].wait()
    for p in range(params):
        rows_ref[p] = jnp.where(inside, gradient_ref[p, 0], 0.0)
    copies[1].wait()
    for b in range(blocks):
        masked = rows_ref[:, b, :].astype(jnp.bfloat16)
        rows_ref[:, b, :] = jnp.dot(masked, basis_ref[0, b], preferred_element_type=jnp.float32)
    for p in range(params):
        payload_ref[p * blocks : (p + 1) * blocks, :] = rows_ref[p].astype(jnp.bfloat16)


def patch_sums(wanted, all_ref, params, blocks):
    members, rows, width = all_ref.shape
    group = 128 // blocks
    tile = 2 * group
    total = jnp.zeros((wanted.shape[0], params * width), jnp.float32)
    for first in (0, rows // 2):
        marks = slice(first + params * blocks, first + rows // 2)
        for start in range(0, members, tile):
            ids = []
            for half in range(start, start + tile, group):
                ids.append(
                    sum(all_ref[m, marks, :].astype(jnp.float32) for m in range(half, half + group))
                )
            ids = jnp.concatenate(ids, axis=1)
            patch = (ids[0:1] * PD + ids[1:2]).astype(jnp.int32)
            hit = jnp.where(wanted == patch, 1.0, 0.0).astype(jnp.bfloat16)
            values = jnp.concatenate(
                [
                    jnp.concatenate(
                        [
                            all_ref[m, first + p * blocks : first + (p + 1) * blocks, :]
                            for m in range(start, start + tile)
                        ],
                        axis=0,
                    )
                    for p in range(params)
                ],
                axis=1,
            )
            total += jnp.dot(hit, values, preferred_element_type=jnp.float32)
    return total


def radial_kernel(up_ref, down_ref, all_ref, to_up_ref, to_down_ref):
    blocks = to_up_ref.shape[0]
    width = all_ref.shape[2]
    params = to_up_ref.shape[1] // width
    wanted = jnp.concatenate(
        [column(up_ref[...], blocks), column(down_ref[...], blocks)], axis=0
    )
    total = patch_sums(wanted, all_ref, params, blocks).astype(jnp.bfloat16)
    to_up_ref[...] = total[:blocks]
    to_down_ref[...] = total[blocks:]


def lateral_kernel(offsets_ref, band_ref, radial_ref, wants_ref, all_ref, out_ref):
    width = all_ref.shape[2]
    params, bands = band_ref.shape
    blocks = out_ref.shape[0] - 8
    patches = all_ref.shape[0] * 2 * PD
    mine = column(wants_ref[...], blocks)
    wanted = [mine]
    for j in range(bands):
        moved = mine + offsets_ref[j]
        moved = jnp.where(moved < 0, moved + patches, moved)
        wanted.append(jnp.where(moved >= patches, moved - patches, moved))
    total = patch_sums(jnp.concatenate(wanted, axis=0), all_ref, params, blocks)
    for p in range(params):
        part = total[:, p * width : (p + 1) * width]
        centre = part[:blocks]
        smooth = centre - (2.0 * radial_ref[p]) * centre
        for j in range(bands):
            shifted = part[(j + 1) * blocks : (j + 2) * blocks]
            smooth = smooth + band_ref[p, j] * (shifted - centre)
        out_ref[:blocks, p * width : (p + 1) * width] = smooth
        out_ref[blocks:, p * width : (p + 1) * width] = jnp.full((8, width), radial_ref[p], jnp.float32)


def expand_kernel(part_ref, up_ref, down_ref, basis_ref, valid_ref, out_ref, rows_ref):
    params, _, blocks, points = out_ref.shape
    width = basis_ref.shape[3]
    neighbours = up_ref[...].astype(jnp.float32) + down_ref[...].astype(jnp.float32)
    smooth = part_ref[:blocks] + part_ref[blocks : blocks + 1] * neighbours
    for p in range(params):
        rows_ref[p] = smooth[:, p * width : (p + 1) * width]
    for b in range(blocks):
        picked = rows_ref[:, b, :].astype(jnp.bfloat16)
        rows_ref[:, b, :] = lax.dot_general(
            picked, basis_ref[0, b], (((1,), (1,)), ((), ())), preferred_element_type=jnp.float32
        )
    inside = inside_mask(valid_ref, blocks, points)
    for p in range(params):
        out_ref[p, 0] = jnp.where(inside, rows_ref[p], 0.0)


VMEM = pl.BlockSpec(memory_space=pltpu.VMEM)
ANY = pl.BlockSpec(memory_space=pl.ANY)
SMEM = pl.BlockSpec(memory_space=pltpu.SMEM)


def call(kernel, ins, out_shape, flops, scratch=()):
    many = isinstance(out_shape, tuple)
    return pl.pallas_call(
        kernel,
        out_shape=out_shape,
        in_specs=list(ins),
        out_specs=(VMEM,) * len(out_shape) if many else VMEM,
        scratch_shapes=list(scratch),
        compiler_params=pltpu.CompilerParams(vmem_limit_bytes=24 * 2**20),
        cost_estimate=pl.CostEstimate(flops=flops, bytes_accessed=2**21, transcendentals=0),
    )


def body(
    gradient, basis, block_owner, block_local, valid_count, band_offsets, band_weight, radial_weight
):
    params, _, blocks, points = gradient.shape
    width = basis.shape[3]
    cuts, rows = lax.axis_size("cuts"), lax.axis_size("group")
    chips = cuts // CORES
    values = params * width
    wants = block_owner[:, :, 0] * PD + block_local
    higher = [(i, i + 1) for i in range(rows - 1)]
    lower = [(j, i) for i, j in higher]
    wants_of_lower = lax.ppermute(wants, "group", higher)
    wants_of_higher = lax.ppermute(wants, "group", lower)
    payload = call(
        project_kernel,
        [ANY] * 2 + [VMEM] * 2,
        jax.ShapeDtypeStruct((params * blocks + ID_ROWS, width), jnp.bfloat16),
        2 * blocks * params * points * width,
        [
            pltpu.VMEM(gradient.shape, gradient.dtype),
            pltpu.VMEM(basis.shape, basis.dtype),
            pltpu.VMEM((params, blocks, width), jnp.float32),
            pltpu.VMEM((ID_ROWS, 128), jnp.int32),
            pltpu.SemaphoreType.DMA((2,)),
        ],
    )(gradient, basis, wants, valid_count)
    partner = [(CORES * z + c, CORES * (z ^ 1) + c) for z in range(chips) for c in range(CORES)]
    pair = jnp.concatenate([payload, lax.ppermute(payload, "cuts", partner)])
    halves = [[CORES * z + c for z in range(h, chips, 2) for c in range(CORES)] for h in range(2)]
    everything = lax.all_gather(pair, "cuts", axis_index_groups=halves)
    piece = jax.ShapeDtypeStruct((blocks, values), jnp.bfloat16)
    to_higher, to_lower = call(
        radial_kernel, [VMEM] * 3, (piece, piece), 4 * blocks * blocks * cuts * values
    )(wants_of_higher, wants_of_lower, everything)
    from_lower = lax.ppermute(to_higher, "group", higher)
    from_higher = lax.ppermute(to_lower, "group", lower)
    part = call(
        lateral_kernel,
        [SMEM] * 3 + [VMEM] * 2,
        jax.ShapeDtypeStruct((blocks + 8, values), jnp.float32),
        10 * blocks * blocks * cuts * values,
    )(band_offsets, band_weight, radial_weight, wants, everything)
    return call(
        expand_kernel,
        [VMEM] * 5,
        jax.ShapeDtypeStruct((params, 1, blocks, points), jnp.float32),
        2 * blocks * params * points * width,
        [pltpu.VMEM((params, blocks, width), jnp.float32)],
    )(part, from_lower, from_higher, basis, valid_count)


def solution(mesh):
    return jax.shard_map(
        body,
        mesh=mesh,
        in_specs=(
            P(None, "group", "cuts", None),
            P("group", "cuts", None, None),
            P("group", "cuts", None),
            P("group", "cuts"),
            P("group", "cuts"),
            P(),
            P(),
            P(),
        ),
        out_specs=P(None, "group", "cuts", None),
        check_vma=False,
    )
```

time: 315 us -> 142 us (0.45)
  waiting for transfers between devices: 218 us -> 98.1 us
  blocking collectives: 54.9 us -> 0 us
  starting transfers between devices: 10.9 us -> 18.7 us
  between operations: 18.6 us -> 13.5 us
  Pallas kernels: 0 us -> 3.65 us
    reduce_scatter x1 -> x0, waiting for transfers between devices: 217 us -> none  [body(): lax.psum_scatter(jnp.dot(onehot.T, projected_gradient, precision=lax.Prec...]
    all_gather x0 -> x1, waiting for transfers between devices: none -> 90.4 us  [body(): everything = lax.all_gather(pair, 'cuts', axis_index_groups=halves)]
    all_gather x1 -> x0, blocking collectives: 54.9 us -> none  [body(): gathered = lax.all_gather(smooth, 'cuts', axis=0, tiled=True)]
    ppermute x4 -> x5, starting transfers between devices: 10.9 us -> 18.7 us  [the longest x1 4.85 us: body(): wants_of_higher = lax.ppermute(wants, 'group', lower)]
    ppermute x4 -> x5, waiting for transfers between devices: 0.92 us -> 7.73 us  [the longest x1 5.6 us: body(): wants_of_lower = lax.ppermute(wants, 'group', higher)]
    unnamed x12 -> x20, local copies, waits for them, and re-layouts: 0.03 us -> 4.15 us
    pallas_call x0 -> x4, Pallas kernels: none -> 3.65 us  [the longest x1 1.3 us: body(): call(expand_kernel, [VMEM] * 5, jax.ShapeDtypeStruct((params, 1, blocks,...]
  transfers between devices with their start and end apart: 5 -> 6, of which waited for: 2 -> 4; matrix products, arithmetic and copies ran while one was open for 1% -> 0% of each run, Pallas kernels for 0% -> 1%
where the time goes in v1:
time: 142 us; the launch traced here: 139 us
  waiting for transfers between devices  98.1 us (69%)
  starting transfers between devices  18.7 us (13%)
  between operations  13.5 us (10%)
  local copies, waits for them, and re-layouts  4.15 us (3%)
  Pallas kernels  3.65 us (3%)
    all_gather x1, waiting for transfers between devices, body(): everything = lax.all_gather(pair, 'cuts', axis_index_groups=halves)  90.4 us
    ppermute x1, waiting for transfers between devices, body(): wants_of_lower = lax.ppermute(wants, 'group', higher)  5.6 us
    ppermute x1, starting transfers between devices, body(): wants_of_higher = lax.ppermute(wants, 'group', lower)  4.85 us
    ppermute x1, starting transfers between devices, body(): from_higher = lax.ppermute(to_lower, 'group', lower)  4.56 us
    unnamed x20, local copies, waits for them, and re-layouts  4.15 us
    ppermute x1, starting transfers between devices, body(): pair = jnp.concatenate([payload, lax.ppermute(payload, 'cuts', partner)])  3.83 us
    ppermute x1, starting transfers between devices, body(): from_lower = lax.ppermute(to_higher, 'group', higher)  3.52 us
  transfers between devices with their start and end apart: 6, of which 4 were waited for; matrix products, arithmetic and copies ran while one was open for 0% of the time, Pallas kernels for 1%

profile of v1, /device:TPU:24, one launch (start us, length us, event | category | flops | bytes accessed | tf_op | source)
XLA Modules:
  0.0 139.4 jit_solution(6352477117168050730)
XLA Ops:
  6.5 0.0 copy-start.8
  6.5 0.0 copy-start.9
  6.5 0.0 all-gather.3.cloned.1.call-start
  6.5 0.7 bitcast_add_fusion.patch_ref.wants_ref
  7.2 0.0 copy-start.2
  7.2 1.2 copy-done.2
  8.5 0.0 copy-start.4
  8.5 0.8 copy-done.4
  9.3 0.0 copy-start.5
  9.3 0.7 copy-done.5
  9.9 0.0 copy-start.7
  9.9 0.6 shard_map.82
  10.6 3.8 %collective-permute-start = (bf16[104,128]{1,0:T(8,128)(2,1)S(1)}, bf16[104,128]{1,0:T(8,128)(2,1)S(1)}, u32[]{:S(2)}, u32[]{:S(2)}) collective-permute-start(bf16[104,128]{1,0:T(8,128)(2,1)S(1)} %shard_map.82), channel_id=1, source_target_pairs={{0,2},{1,3},{2,0},{3,1},{4,6},{5,7},{6,4},{7,5},{8,10},{9,11},{10,... | collective-permute-start | bytes 79880 | tf_op jit(solution)/shard_map/ppermute | solution.py:186
  14.4 1.9 %collective-permute-done = bf16[104,128]{1,0:T(8,128)(2,1)S(1)} collective-permute-done((bf16[104,128]{1,0:T(8,128)(2,1)S(1)}, bf16[104,128]{1,0:T(8,128)(2,1)S(1)}, u32[]{:S(2)}, u32[]{:S(2)}) %collective-permute-start) | collective-permute-done | bytes 26656 | tf_op jit(solution)/shard_map/ppermute | solution.py:186
  16.3 0.6 pad_maximum_fusion
  16.9 0.0 all-gather.3.cloned.1.call-update
  17.0 4.8 %collective-permute-start.1 = (s32[1,32]{1,0:T(1,128)S(1)}, s32[1,32]{1,0:T(1,128)S(1)}, u32[]{:S(2)}, u32[]{:S(2)}) collective-permute-start(s32[1,32]{1,0:T(1,128)S(1)} %bitcast_add_fusion.patch_ref.wants_ref), channel_id=1, source_target_pairs={{64,0},{128,64},{192,128},{256,192},{320,256},{384,320},{448,384},... | collective-permute-start | bytes 392 | tf_op jit(solution)/shard_map/ppermute | solution.py:171
  21.8 1.9 %collective-permute-start.2 = (s32[1,32]{1,0:T(1,128)S(1)}, s32[1,32]{1,0:T(1,128)S(1)}, u32[]{:S(2)}, u32[]{:S(2)}) collective-permute-start(s32[1,32]{1,0:T(1,128)S(1)} %bitcast_add_fusion.patch_ref.wants_ref), channel_id=1, source_target_pairs={{0,64},{64,128},{128,192},{192,256},{256,320},{320,384},{384,448},... | collective-permute-start | bytes 392 | tf_op jit(solution)/shard_map/ppermute | solution.py:170
  23.7 0.0 collective-permute-done.1.up_ref
  23.8 5.6 %collective-permute-done.2.down_ref = s32[1,32]{1,0:T(1,128)S(1)} collective-permute-done((s32[1,32]{1,0:T(1,128)S(1)}, s32[1,32]{1,0:T(1,128)S(1)}, u32[]{:S(2)}, u32[]{:S(2)}) %collective-permute-start.2) | collective-permute-done | bytes 160 | tf_op jit(solution)/shard_map/ppermute | solution.py:170
  29.4 90.4 %all-gather.3.cloned.1.call-done = bf16[6656,128]{1,0:T(8,128)(2,1)} async-done(((bf16[208,128]{1,0:T(8,128)(2,1)}), bf16[6656,128]{1,0:T(8,128)(2,1)}) %all-gather.3.cloned.1.call-update) | async-done | bytes 1703952 | tf_op jit(solution)/shard_map/all_gather | solution.py:188
  119.7 0.0 copy-start
  119.7 1.5 %copy-done = bf16[6656,128]{1,0:T(8,128)(2,1)S(1)} copy-done((bf16[6656,128]{1,0:T(8,128)(2,1)S(1)}, bf16[6656,128]{1,0:T(8,128)(2,1)}, u32[]{:S(2)}) %copy-start) | copy-done | bytes 1703960
  121.2 0.0 copy-start.1
  121.2 0.0 copy-start.3
  121.2 0.0 copy-start.6
  121.2 0.5 shard_map.84
  121.7 3.5 %collective-permute-start.3 = (bf16[32,384]{1,0:T(8,128)(2,1)S(1)}, bf16[32,384]{1,0:T(8,128)(2,1)S(1)}, u32[]{:S(2)}, u32[]{:S(2)}) collective-permute-start(bf16[32,384]{1,0:T(8,128)(2,1)S(1)} %get-tuple-element.7), channel_id=1, source_target_pairs={{0,64},{64,128},{128,192},{192,256},{256,320},{320,384},{384,448},... | collective-permute-start | bytes 73736 | tf_op jit(solution)/shard_map/ppermute | solution.py:193
  125.2 4.6 %collective-permute-start.4 = (bf16[32,384]{1,0:T(8,128)(2,1)S(1)}, bf16[32,384]{1,0:T(8,128)(2,1)S(1)}, u32[]{:S(2)}, u32[]{:S(2)}) collective-permute-start(bf16[32,384]{1,0:T(8,128)(2,1)S(1)} %get-tuple-element.8), channel_id=1, source_target_pairs={{64,0},{128,64},{192,128},{256,192},{320,256},{384,320},{448,384},... | collective-permute-start | bytes 73736 | tf_op jit(solution)/shard_map/ppermute | solution.py:194
  129.8 0.0 copy-done.8
  129.8 0.0 copy-done.9
  129.8 0.0 copy-done.7
  129.8 0.0 copy-done.1
  129.8 1.2 shard_map.83.part_ref
  131.1 0.0 collective-permute-done.3.up_ref
  131.1 0.2 collective-permute-done.4.down_ref
  131.3 0.0 copy-done.3
  131.3 0.0 copy-done.6
  131.3 1.3 shard_map.85
Async XLA Ops:
  6.5 123.2 %copy-start.8 = (s32[4]{0:T(128)S(1)}, s32[4]{0:T(128)}, u32[]{:S(2)}) copy-start(s32[4]{0:T(128)} %offsets_ref.1) | copy-start | bytes 52
  6.5 123.3 %copy-start.9 = (f32[3]{0:T(128)S(1)}, f32[3]{0:T(128)}, u32[]{:S(2)}) copy-start(f32[3]{0:T(128)} %radial_ref.1) | copy-start | bytes 40
  6.5 113.2 %all-gather.3.cloned.1.call-start = ((), (), s32[]{:S(2)}) async-start(), calls=%async_computation | async-start | bytes 1757184 | tf_op jit(solution)/shard_map/all_gather | solution.py:188
  7.2 1.2 copy-start.2
  8.5 0.8 copy-start.4
  9.3 0.7 copy-start.5
  9.9 119.9 %copy-start.7 = (f32[3,4]{1,0:T(4,128)S(1)}, f32[3,4]{1,0:T(4,128)}, u32[]{:S(2)}) copy-start(f32[3,4]{1,0:T(4,128)} %band_ref.1) | copy-start | bytes 148
  10.6 5.7 %collective-permute-start = (bf16[104,128]{1,0:T(8,128)(2,1)S(1)}, bf16[104,128]{1,0:T(8,128)(2,1)S(1)}, u32[]{:S(2)}, u32[]{:S(2)}) collective-permute-start(bf16[104,128]{1,0:T(8,128)(2,1)S(1)} %shard_map.82), channel_id=1, source_target_pairs={{0,2},{1,3},{2,0},{3,1},{4,6},{5,7},{6,4},{7,5},{8,10},{9,11},{10,... | collective-permute-start | bytes 79880 | tf_op jit(solution)/shard_map/ppermute | solution.py:186
  17.0 6.8 %collective-permute-start.1 = (s32[1,32]{1,0:T(1,128)S(1)}, s32[1,32]{1,0:T(1,128)S(1)}, u32[]{:S(2)}, u32[]{:S(2)}) collective-permute-start(s32[1,32]{1,0:T(1,128)S(1)} %bitcast_add_fusion.patch_ref.wants_ref), channel_id=1, source_target_pairs={{64,0},{128,64},{192,128},{256,192},{320,256},{384,320},{448,384},... | collective-permute-start | bytes 392 | tf_op jit(solution)/shard_map/ppermute | solution.py:171
  21.8 7.5 %collective-permute-start.2 = (s32[1,32]{1,0:T(1,128)S(1)}, s32[1,32]{1,0:T(1,128)S(1)}, u32[]{:S(2)}, u32[]{:S(2)}) collective-permute-start(s32[1,32]{1,0:T(1,128)S(1)} %bitcast_add_fusion.patch_ref.wants_ref), channel_id=1, source_target_pairs={{0,64},{64,128},{128,192},{192,256},{256,320},{320,384},{384,448},... | collective-permute-start | bytes 392 | tf_op jit(solution)/shard_map/ppermute | solution.py:170
  119.7 1.5 %copy-start = (bf16[6656,128]{1,0:T(8,128)(2,1)S(1)}, bf16[6656,128]{1,0:T(8,128)(2,1)}, u32[]{:S(2)}) copy-start(bf16[6656,128]{1,0:T(8,128)(2,1)} %all-gather.3.cloned.1.call-done) | copy-start | bytes 5111812
  121.2 8.6 %copy-start.1 = (bf16[6656,128]{1,0:T(8,128)(2,1)S(1)}, bf16[6656,128]{1,0:T(8,128)(2,1)}, u32[]{:S(2)}) copy-start(bf16[6656,128]{1,0:T(8,128)(2,1)} %all-gather.3.cloned.1.call-done) | copy-start | bytes 5111812
  121.2 10.1 %copy-start.3 = (bf16[1,32,128,128]{3,2,1,0:T(8,128)(2,1)S(1)}, bf16[1,32,128,128]{3,2,1,0:T(8,128)(2,1)}, u32[]{:S(2)}) copy-start(bf16[1,32,128,128]{3,2,1,0:T(8,128)(2,1)} %basis_ref.1) | copy-start | bytes 3145732
  121.2 10.1 %copy-start.6 = (s32[1,32]{1,0:T(1,128)S(1)}, s32[1,32]{1,0:T(1,128)}, u32[]{:S(2)}) copy-start(s32[1,32]{1,0:T(1,128)} %valid_ref.3) | copy-start | bytes 388
  121.7 9.4 %collective-permute-start.3 = (bf16[32,384]{1,0:T(8,128)(2,1)S(1)}, bf16[32,384]{1,0:T(8,128)(2,1)S(1)}, u32[]{:S(2)}, u32[]{:S(2)}) collective-permute-start(bf16[32,384]{1,0:T(8,128)(2,1)S(1)} %get-tuple-element.7), channel_id=1, source_target_pairs={{0,64},{64,128},{128,192},{192,256},{256,320},{320,384},{384,448},... | collective-permute-start | bytes 73736 | tf_op jit(solution)/shard_map/ppermute | solution.py:193
  125.2 6.1 %collective-permute-start.4 = (bf16[32,384]{1,0:T(8,128)(2,1)S(1)}, bf16[32,384]{1,0:T(8,128)(2,1)S(1)}, u32[]{:S(2)}, u32[]{:S(2)}) collective-permute-start(bf16[32,384]{1,0:T(8,128)(2,1)S(1)} %get-tuple-element.8), channel_id=1, source_target_pairs={{64,0},{128,64},{192,128},{256,192},{320,256},{384,320},{448,384},... | collective-permute-start | bytes 73736 | tf_op jit(solution)/shard_map/ppermute | solution.py:194
Sparse Core Ops, SparseCore 0:
  17.1 102.5 all-gather.2

commit v2 on v1

--- a/solution.py
+++ b/solution.py
@@ -54,56 +54,54 @@
 
 
 def patch_sums(wanted, all_ref, params, blocks):
-    members, rows, width = all_ref.shape
+    members, _, width = all_ref.shape
     group = 128 // blocks
     tile = 2 * group
     total = jnp.zeros((wanted.shape[0], params * width), jnp.float32)
-    for first in (0, rows // 2):
-        marks = slice(first + params * blocks, first + rows // 2)
-        for start in range(0, members, tile):
-            ids = []
-            for half in range(start, start + tile, group):
-                ids.append(
-                    sum(all_ref[m, marks, :].astype(jnp.float32) for m in range(half, half + group))
+    for start in range(0, members, tile):
+        ids = []
+        for half in range(start, start + tile, group):
+            ids.append(
+                sum(all_ref[m, params * blocks :, :].astype(jnp.float32) for m in range(half, half + group))
+            )
+        ids = jnp.concatenate(ids, axis=1)
+        patch = (ids[0:1] * PD + ids[1:2]).astype(jnp.int32)
+        hit = jnp.where(wanted == patch, 1.0, 0.0).astype(jnp.bfloat16)
+        values = jnp.concatenate(
+            [
+                jnp.concatenate(
+                    [all_ref[m, p * blocks : (p + 1) * blocks, :] for m in range(start, start + tile)],
+                    axis=0,
                 )
-            ids = jnp.concatenate(ids, axis=1)
-            patch = (ids[0:1] * PD + ids[1:2]).astype(jnp.int32)
-            hit = jnp.where(wanted == patch, 1.0, 0.0).astype(jnp.bfloat16)
-            values = jnp.concatenate(
-                [
-                    jnp.concatenate(
-                        [
-                            all_ref[m, first + p * blocks : first + (p + 1) * blocks, :]
-                            for m in range(start, start + tile)
-                        ],
-                        axis=0,
-                    )
-                    for p in range(params)
-                ],
-                axis=1,
-            )
-            total += jnp.dot(hit, values, preferred_element_type=jnp.float32)
+                for p in range(params)
+            ],
+            axis=1,
+        )
+        total += jnp.dot(hit, values, preferred_element_type=jnp.float32)
     return total
 
 
+def columns(ref, blocks):
+    return [column(ref[i : i + 1, :], blocks) for i in range(ref.shape[0])]
+
+
 def radial_kernel(up_ref, down_ref, all_ref, to_up_ref, to_down_ref):
-    blocks = to_up_ref.shape[0]
-    width = all_ref.shape[2]
-    params = to_up_ref.shape[1] // width
-    wanted = jnp.concatenate(
-        [column(up_ref[...], blocks), column(down_ref[...], blocks)], axis=0
-    )
+    count = to_up_ref.shape[0]
+    blocks = count // up_ref.shape[0]
+    params = to_up_ref.shape[1] // all_ref.shape[2]
+    wanted = jnp.concatenate(columns(up_ref, blocks) + columns(down_ref, blocks), axis=0)
     total = patch_sums(wanted, all_ref, params, blocks).astype(jnp.bfloat16)
-    to_up_ref[...] = total[:blocks]
-    to_down_ref[...] = total[blocks:]
+    to_up_ref[...] = total[:count]
+    to_down_ref[...] = total[count:]
 
 
 def lateral_kernel(offsets_ref, band_ref, radial_ref, wants_ref, all_ref, out_ref):
     width = all_ref.shape[2]
     params, bands = band_ref.shape
-    blocks = out_ref.shape[0] - 8
+    count = out_ref.shape[0] - 8
+    blocks = count // wants_ref.shape[0]
     patches = all_ref.shape[0] * 2 * PD
-    mine = column(wants_ref[...], blocks)
+    mine = jnp.concatenate(columns(wants_ref, blocks), axis=0)
     wanted = [mine]
     for j in range(bands):
         moved = mine + offsets_ref[j]
@@ -112,20 +110,31 @@
     total = patch_sums(jnp.concatenate(wanted, axis=0), all_ref, params, blocks)
     for p in range(params):
         part = total[:, p * width : (p + 1) * width]
-        centre = part[:blocks]
+        centre = part[:count]
         smooth = centre - (2.0 * radial_ref[p]) * centre
         for j in range(bands):
-            shifted = part[(j + 1) * blocks : (j + 2) * blocks]
+            shifted = part[(j + 1) * count : (j + 2) * count]
             smooth = smooth + band_ref[p, j] * (shifted - centre)
-        out_ref[:blocks, p * width : (p + 1) * width] = smooth
-        out_ref[blocks:, p * width : (p + 1) * width] = jnp.full((8, width), radial_ref[p], jnp.float32)
-
-
-def expand_kernel(part_ref, up_ref, down_ref, basis_ref, valid_ref, out_ref, rows_ref):
+        out_ref[:count, p * width : (p + 1) * width] = smooth
+        out_ref[count:, p * width : (p + 1) * width] = jnp.full((8, width), radial_ref[p], jnp.float32)
+
+
+def radial_added(part_ref, up_ref, down_ref, first, blocks):
+    count = up_ref.shape[0]
+    rows = slice(first, first + blocks)
+    neighbours = up_ref[rows, :].astype(jnp.float32) + down_ref[rows, :].astype(jnp.float32)
+    return part_ref[rows, :] + part_ref[count : count + 1, :] * neighbours
+
+
+def partner_kernel(part_ref, up_ref, down_ref, out_ref):
+    blocks = out_ref.shape[0]
+    out_ref[...] = radial_added(part_ref, up_ref, down_ref, blocks, blocks).astype(out_ref.dtype)
+
+
+def expand_kernel(part_ref, up_ref, down_ref, other_ref, basis_ref, valid_ref, out_ref, rows_ref):
     params, _, blocks, points = out_ref.shape
     width = basis_ref.shape[3]
-    neighbours = up_ref[...].astype(jnp.float32) + down_ref[...].astype(jnp.float32)
-    smooth = part_ref[:blocks] + part_ref[blocks : blocks + 1] * neighbours
+    smooth = radial_added(part_ref, up_ref, down_ref, 0, blocks) + other_ref[...].astype(jnp.float32)
     for p in range(params):
         rows_ref[p] = smooth[:, p * width : (p + 1) * width]
     for b in range(blocks):
@@ -139,7 +148,7 @@
 
 
 VMEM = pl.BlockSpec(memory_space=pltpu.VMEM)
-ANY = pl.BlockSpec(memory_space=pl.ANY)
+HBM = pl.BlockSpec(memory_space=pltpu.HBM)
 SMEM = pl.BlockSpec(memory_space=pltpu.SMEM)
 
 
@@ -164,14 +173,16 @@
     cuts, rows = lax.axis_size("cuts"), lax.axis_size("group")
     chips = cuts // CORES
     values = params * width
-    wants = block_owner[:, :, 0] * PD + block_local
+    partner = [(CORES * z + c, CORES * (z ^ 1) + c) for z in range(chips) for c in range(CORES)]
     higher = [(i, i + 1) for i in range(rows - 1)]
     lower = [(j, i) for i, j in higher]
+    own = block_owner[:, :, 0] * PD + block_local
+    wants = jnp.concatenate([own, lax.ppermute(own, "cuts", partner)])
     wants_of_lower = lax.ppermute(wants, "group", higher)
     wants_of_higher = lax.ppermute(wants, "group", lower)
     payload = call(
         project_kernel,
-        [ANY] * 2 + [VMEM] * 2,
+        [HBM] * 2 + [VMEM] * 2,
         jax.ShapeDtypeStruct((params * blocks + ID_ROWS, width), jnp.bfloat16),
         2 * blocks * params * points * width,
         [
@@ -181,30 +192,33 @@
             pltpu.VMEM((ID_ROWS, 128), jnp.int32),
             pltpu.SemaphoreType.DMA((2,)),
         ],
-    )(gradient, basis, wants, valid_count)
-    partner = [(CORES * z + c, CORES * (z ^ 1) + c) for z in range(chips) for c in range(CORES)]
-    pair = jnp.concatenate([payload, lax.ppermute(payload, "cuts", partner)])
+    )(gradient, basis, own, valid_count)
     halves = [[CORES * z + c for z in range(h, chips, 2) for c in range(CORES)] for h in range(2)]
-    everything = lax.all_gather(pair, "cuts", axis_index_groups=halves)
-    piece = jax.ShapeDtypeStruct((blocks, values), jnp.bfloat16)
-    to_higher, to_lower = call(
-        radial_kernel, [VMEM] * 3, (piece, piece), 4 * blocks * blocks * cuts * values
-    )(wants_of_higher, wants_of_lower, everything)
+    gathered = lax.all_gather(payload, "cuts", axis_index_groups=halves)
+    piece = jax.ShapeDtypeStruct((2 * blocks, values), jnp.bfloat16)
+    one_hot = blocks * blocks * cuts * values
+    to_higher, to_lower = call(radial_kernel, [VMEM] * 3, (piece, piece), 4 * one_hot)(
+        wants_of_higher, wants_of_lower, gathered
+    )
     from_lower = lax.ppermute(to_higher, "group", higher)
     from_higher = lax.ppermute(to_lower, "group", lower)
     part = call(
         lateral_kernel,
         [SMEM] * 3 + [VMEM] * 2,
-        jax.ShapeDtypeStruct((blocks + 8, values), jnp.float32),
-        10 * blocks * blocks * cuts * values,
-    )(band_offsets, band_weight, radial_weight, wants, everything)
+        jax.ShapeDtypeStruct((2 * blocks + 8, values), jnp.float32),
+        10 * one_hot,
+    )(band_offsets, band_weight, radial_weight, wants, gathered)
+    for_partner = call(
+        partner_kernel, [VMEM] * 3, jax.ShapeDtypeStruct((blocks, values), jnp.bfloat16), blocks * values
+    )(part, from_lower, from_higher)
+    from_partner = lax.ppermute(for_partner, "cuts", partner)
     return call(
         expand_kernel,
-        [VMEM] * 5,
+        [VMEM] * 6,
         jax.ShapeDtypeStruct((params, 1, blocks, points), jnp.float32),
         2 * blocks * params * points * width,
         [pltpu.VMEM((params, blocks, width), jnp.float32)],
-    )(part, from_lower, from_higher, basis, valid_count)
+    )(part, from_lower, from_higher, from_partner, basis, valid_count)
 
 
 def solution(mesh):

time: 142 us -> 82.5 us (0.58)
  the two profiles are of different devices: /device:TPU:24 before, /device:TPU:22 now
where the time goes in v2:
time: 82.5 us; the launch traced here: 82.1 us
  blocking collectives  49.4 us (60%)
  starting transfers between devices  21.2 us (26%)
  waiting for transfers between devices  4.97 us (6%)
  Pallas kernels  3.62 us (4%)
  local copies, waits for them, and re-layouts  2.04 us (2%)
    all_gather x1, blocking collectives, body(): gathered = lax.all_gather(payload, 'cuts', axis_index_groups=halves)  49.4 us
    ppermute x1, starting transfers between devices, body(): wants_of_lower = lax.ppermute(wants, 'group', higher)  5.22 us
    ppermute x1, starting transfers between devices, body(): from_higher = lax.ppermute(to_lower, 'group', lower)  3.92 us
    ppermute x1, starting transfers between devices, body(): wants = jnp.concatenate([own, lax.ppermute(own, 'cuts', partner)])  3.81 us
    ppermute x1, starting transfers between devices, body(): from_partner = lax.ppermute(for_partner, 'cuts', partner)  3.63 us
    ppermute x1, waiting for transfers between devices, body(): from_higher = lax.ppermute(to_lower, 'group', lower)  2.88 us
    ppermute x1, starting transfers between devices, body(): wants_of_higher = lax.ppermute(wants, 'group', lower)  2.74 us
    ppermute x1, waiting for transfers between devices, body(): from_partner = lax.ppermute(for_partner, 'cuts', partner)  2.08 us
  transfers between devices with their start and end apart: 6, of which 2 were waited for; matrix products, arithmetic and copies ran while one was open for 0% of the time, Pallas kernels for 2%

profile of v2, /device:TPU:22, one launch (start us, length us, event | category | flops | bytes accessed | tf_op | source)
XLA Modules:
  0.0 82.1 jit_solution(10547962331228423306)
XLA Ops:
  0.0 0.0 copy-start.3
  0.0 0.7 bitcast_add_fusion.patch_ref
  0.7 3.8 %collective-permute-start = (s32[1,32]{1,0:T(1,128)S(1)}, s32[1,32]{1,0:T(1,128)S(1)}, u32[]{:S(2)}, u32[]{:S(2)}) collective-permute-start(s32[1,32]{1,0:T(1,128)S(1)} %bitcast_add_fusion.patch_ref), channel_id=1, source_target_pairs={{0,2},{1,3},{2,0},{3,1},{4,6},{5,7},{6,4},{7,5},{8,10},{9,11},{10,... | collective-permute-start | bytes 392 | tf_op jit(solution)/shard_map/ppermute | solution.py:180
  4.5 0.0 copy-done.3
  4.5 0.0 copy-start
  4.5 1.2 %copy-done = bf16[1,32,128,128]{3,2,1,0:T(8,128)(2,1)S(1)} copy-done((bf16[1,32,128,128]{3,2,1,0:T(8,128)(2,1)S(1)}, bf16[1,32,128,128]{3,2,1,0:T(8,128)(2,1)}, u32[]{:S(2)}) %copy-start) | copy-done | bytes 1048600
  5.8 0.0 copy-start.2
  5.8 0.8 copy-done.2
  6.5 0.6 shard_map.82
  7.2 0.0 collective-permute-done
  7.2 2.7 %collective-permute-start.1 = (s32[2,32]{1,0:T(2,128)S(1)}, s32[2,32]{1,0:T(2,128)S(1)}, u32[]{:S(2)}, u32[]{:S(2)}) collective-permute-start(s32[2,32]{1,0:T(2,128)S(1)} %pad_add_fusion.wants_ref), channel_id=1, source_target_pairs={{64,0},{128,64},{192,128},{256,192},{320,256},{384,320},{448,384},... | collective-permute-start | bytes 776 | tf_op jit(solution)/shard_map/ppermute | solution.py:182
  9.9 5.2 %collective-permute-start.2 = (s32[2,32]{1,0:T(2,128)S(1)}, s32[2,32]{1,0:T(2,128)S(1)}, u32[]{:S(2)}, u32[]{:S(2)}) collective-permute-start(s32[2,32]{1,0:T(2,128)S(1)} %pad_add_fusion.wants_ref), channel_id=1, source_target_pairs={{0,64},{64,128},{128,192},{192,256},{256,320},{320,384},{384,448},... | collective-permute-start | bytes 776 | tf_op jit(solution)/shard_map/ppermute | solution.py:181
  15.2 0.0 copy-start.4
  15.2 0.0 copy-start.5
  15.2 0.0 copy-start.6
  15.2 49.4 %all-gather = bf16[3328,128]{1,0:T(8,128)(2,1)S(1)} all-gather(bf16[104,128]{1,0:T(8,128)(2,1)S(1)} %shard_map.82), channel_id=2, replica_groups={{0,1,4,5,8,9,12,13,16,17,20,21,24,25,28,29,32,33,36,37,40,41,44,45,48,4..., dimensions={0}, use_global_device_ids=true | all-gather | bytes 878592 | tf_op jit(solution)/shard_map/all_gather | solution.py:197
  64.6 0.0 copy-start.1
  64.6 0.0 collective-permute-done.1.up_ref
  64.6 0.0 collective-permute-done.2.down_ref
  64.6 0.4 shard_map.84
  65.1 1.9 %collective-permute-start.3 = (bf16[64,384]{1,0:T(8,128)(2,1)S(1)}, bf16[64,384]{1,0:T(8,128)(2,1)S(1)}, u32[]{:S(2)}, u32[]{:S(2)}) collective-permute-start(bf16[64,384]{1,0:T(8,128)(2,1)S(1)} %get-tuple-element.7), channel_id=1, source_target_pairs={{0,64},{64,128},{128,192},{192,256},{256,320},{320,384},{384,448},... | collective-permute-start | bytes 147464 | tf_op jit(solution)/shard_map/ppermute | solution.py:203
  67.0 3.9 %collective-permute-start.4 = (bf16[64,384]{1,0:T(8,128)(2,1)S(1)}, bf16[64,384]{1,0:T(8,128)(2,1)S(1)}, u32[]{:S(2)}, u32[]{:S(2)}) collective-permute-start(bf16[64,384]{1,0:T(8,128)(2,1)S(1)} %get-tuple-element.8), channel_id=1, source_target_pairs={{64,0},{128,64},{192,128},{256,192},{320,256},{384,320},{448,384},... | collective-permute-start | bytes 147464 | tf_op jit(solution)/shard_map/ppermute | solution.py:204
  70.9 0.0 copy-done.4
  70.9 0.0 copy-done.5
  70.9 0.0 copy-done.6
  70.9 1.2 %shard_map.83.part_ref = f32[72,384]{1,0:T(8,128)S(1)} custom-call(s32[4]{0:T(128)S(1)} %copy-done.5, f32[3,4]{1,0:T(4,128)S(1)} %copy-done.4, f32[3]{0:T(128)S(1)} %copy-done.6, s32[2,32]{1,0:T(2,128)S(1)} %pad_add_fusion.wants_ref, bf16[32,104,128]{2,1,0:T(8,128)(2,1)S(1)} %bitcast.4), custom_call_target="tpu_custom_call" | custom-call | flops 251658240 | bytes 2097152 | tf_op jit(solution)/shard_map/pallas_call | solution.py:205
  72.2 0.0 collective-permute-done.3.up_ref
  72.2 2.9 %collective-permute-done.4.down_ref = bf16[64,384]{1,0:T(8,128)(2,1)S(1)} collective-permute-done((bf16[64,384]{1,0:T(8,128)(2,1)S(1)}, bf16[64,384]{1,0:T(8,128)(2,1)S(1)}, u32[]{:S(2)}, u32[]{:S(2)}) %collective-permute-start.4) | collective-permute-done | bytes 49184 | tf_op jit(solution)/shard_map/ppermute | solution.py:204
  75.1 3.6 %collective-permute-start.5 = (bf16[32,384]{1,0:T(8,128)(2,1)S(1)}, bf16[32,384]{1,0:T(8,128)(2,1)S(1)}, u32[]{:S(2)}, u32[]{:S(2)}) collective-permute-start(bf16[32,384]{1,0:T(8,128)(2,1)S(1)} %shard_map.85), channel_id=1, source_target_pairs={{0,2},{1,3},{2,0},{3,1},{4,6},{5,7},{6,4},{7,5},{8,10},{9,11},{10,... | collective-permute-start | bytes 73736 | tf_op jit(solution)/shard_map/ppermute | solution.py:214
  78.7 2.1 %collective-permute-done.5.other_ref = bf16[32,384]{1,0:T(8,128)(2,1)S(1)} collective-permute-done((bf16[32,384]{1,0:T(8,128)(2,1)S(1)}, bf16[32,384]{1,0:T(8,128)(2,1)S(1)}, u32[]{:S(2)}, u32[]{:S(2)}) %collective-permute-start.5) | collective-permute-done | bytes 24608 | tf_op jit(solution)/shard_map/ppermute | solution.py:214
  80.8 0.0 copy-done.1
  80.8 1.3 %shard_map.86 = f32[3,1,32,128]{3,2,1,0:T(8,128)} custom-call(f32[72,384]{1,0:T(8,128)S(1)} %shard_map.83.part_ref, bf16[64,384]{1,0:T(8,128)(2,1)S(1)} %collective-permute-done.3.up_ref, bf16[64,384]{1,0:T(8,128)(2,1)S(1)} %collective-permute-done.4.down_ref, bf16[32,384]{1,0:T(8,128)(2,1)S(1)} %collective-permute-done.5.other_ref, ...), custom_call_target="tpu_custom_call" | custom-call | flops 3145728 | bytes 2097152 | tf_op jit(solution)/shard_map/pallas_call | solution.py:215
  (2 shorter events, 0.0 us)
Async XLA Ops:
  0.0 4.5 %copy-start.3 = (s32[1,32]{1,0:T(1,128)S(1)}, s32[1,32]{1,0:T(1,128)}, u32[]{:S(2)}) copy-start(s32[1,32]{1,0:T(1,128)} %valid_ref.3) | copy-start | bytes 388
  0.7 6.5 %collective-permute-start = (s32[1,32]{1,0:T(1,128)S(1)}, s32[1,32]{1,0:T(1,128)S(1)}, u32[]{:S(2)}, u32[]{:S(2)}) collective-permute-start(s32[1,32]{1,0:T(1,128)S(1)} %bitcast_add_fusion.patch_ref), channel_id=1, source_target_pairs={{0,2},{1,3},{2,0},{3,1},{4,6},{5,7},{6,4},{7,5},{8,10},{9,11},{10,... | collective-permute-start | bytes 392 | tf_op jit(solution)/shard_map/ppermute | solution.py:180
  4.5 1.2 %copy-start = (bf16[1,32,128,128]{3,2,1,0:T(8,128)(2,1)S(1)}, bf16[1,32,128,128]{3,2,1,0:T(8,128)(2,1)}, u32[]{:S(2)}) copy-start(bf16[1,32,128,128]{3,2,1,0:T(8,128)(2,1)} %basis_ref.1) | copy-start | bytes 3145732
  5.8 0.8 copy-start.2
  7.2 57.4 %collective-permute-start.1 = (s32[2,32]{1,0:T(2,128)S(1)}, s32[2,32]{1,0:T(2,128)S(1)}, u32[]{:S(2)}, u32[]{:S(2)}) collective-permute-start(s32[2,32]{1,0:T(2,128)S(1)} %pad_add_fusion.wants_ref), channel_id=1, source_target_pairs={{64,0},{128,64},{192,128},{256,192},{320,256},{384,320},{448,384},... | collective-permute-start | bytes 776 | tf_op jit(solution)/shard_map/ppermute | solution.py:182
  9.9 54.7 %collective-permute-start.2 = (s32[2,32]{1,0:T(2,128)S(1)}, s32[2,32]{1,0:T(2,128)S(1)}, u32[]{:S(2)}, u32[]{:S(2)}) collective-permute-start(s32[2,32]{1,0:T(2,128)S(1)} %pad_add_fusion.wants_ref), channel_id=1, source_target_pairs={{0,64},{64,128},{128,192},{192,256},{256,320},{320,384},{384,448},... | collective-permute-start | bytes 776 | tf_op jit(solution)/shard_map/ppermute | solution.py:181
  15.2 55.8 %copy-start.4 = (f32[3,4]{1,0:T(4,128)S(1)}, f32[3,4]{1,0:T(4,128)}, u32[]{:S(2)}) copy-start(f32[3,4]{1,0:T(4,128)} %band_ref.1) | copy-start | bytes 148
  15.2 55.8 %copy-start.5 = (s32[4]{0:T(128)S(1)}, s32[4]{0:T(128)}, u32[]{:S(2)}) copy-start(s32[4]{0:T(128)} %offsets_ref.1) | copy-start | bytes 52
  15.2 55.7 %copy-start.6 = (f32[3]{0:T(128)S(1)}, f32[3]{0:T(128)}, u32[]{:S(2)}) copy-start(f32[3]{0:T(128)} %radial_ref.1) | copy-start | bytes 40
  64.6 16.2 %copy-start.1 = (bf16[1,32,128,128]{3,2,1,0:T(8,128)(2,1)S(1)}, bf16[1,32,128,128]{3,2,1,0:T(8,128)(2,1)}, u32[]{:S(2)}) copy-start(bf16[1,32,128,128]{3,2,1,0:T(8,128)(2,1)} %basis_ref.1) | copy-start | bytes 3145732
  65.1 7.1 %collective-permute-start.3 = (bf16[64,384]{1,0:T(8,128)(2,1)S(1)}, bf16[64,384]{1,0:T(8,128)(2,1)S(1)}, u32[]{:S(2)}, u32[]{:S(2)}) collective-permute-start(bf16[64,384]{1,0:T(8,128)(2,1)S(1)} %get-tuple-element.7), channel_id=1, source_target_pairs={{0,64},{64,128},{128,192},{192,256},{256,320},{320,384},{384,448},... | collective-permute-start | bytes 147464 | tf_op jit(solution)/shard_map/ppermute | solution.py:203
  67.0 8.1 %collective-permute-start.4 = (bf16[64,384]{1,0:T(8,128)(2,1)S(1)}, bf16[64,384]{1,0:T(8,128)(2,1)S(1)}, u32[]{:S(2)}, u32[]{:S(2)}) collective-permute-start(bf16[64,384]{1,0:T(8,128)(2,1)S(1)} %get-tuple-element.8), channel_id=1, source_target_pairs={{64,0},{128,64},{192,128},{256,192},{320,256},{384,320},{448,384},... | collective-permute-start | bytes 147464 | tf_op jit(solution)/shard_map/ppermute | solution.py:204
  75.1 5.7 %collective-permute-start.5 = (bf16[32,384]{1,0:T(8,128)(2,1)S(1)}, bf16[32,384]{1,0:T(8,128)(2,1)S(1)}, u32[]{:S(2)}, u32[]{:S(2)}) collective-permute-start(bf16[32,384]{1,0:T(8,128)(2,1)S(1)} %shard_map.85), channel_id=1, source_target_pairs={{0,2},{1,3},{2,0},{3,1},{4,6},{5,7},{6,4},{7,5},{8,10},{9,11},{10,... | collective-permute-start | bytes 73736 | tf_op jit(solution)/shard_map/ppermute | solution.py:214

commit v3 on v2

--- a/solution.py
+++ b/solution.py
@@ -24,8 +24,12 @@
     return lax.broadcasted_iota(jnp.int32, (blocks, points), 1) < count
 
 
+def quarter(position):
+    return (position // (2 * CORES)) % 2 * CORES + position % CORES
+
+
 def project_kernel(
-    gradient_hbm, basis_hbm, patch_ref, valid_ref, payload_ref, gradient_ref, basis_ref, rows_ref, ids_ref, done
+    gradient_hbm, basis_hbm, patch_ref, valid_ref, other_ref, up_ref, down_ref, payload_ref, known_ref, gradient_ref, basis_ref, rows_ref, ids_ref, done
 ):
     copies = [
         pltpu.make_async_copy(gradient_hbm, gradient_ref, done.at[0]),
@@ -38,9 +42,12 @@
     ids_ref[...] = jnp.zeros_like(ids_ref)
     ids_ref[0:1, 0:blocks] = patch_ref[...] // PD
     ids_ref[1:2, 0:blocks] = patch_ref[...] % PD
-    position = lax.axis_index("cuts")
-    quarter = (position // (2 * CORES)) % 2 * CORES + position % CORES
-    ids = pltpu.roll(ids_ref[...].astype(jnp.float32), quarter * blocks, 1)
+    known_ref[0:1, :] = patch_ref[...]
+    known_ref[1:2, :] = other_ref[...]
+    known_ref[2:4, :] = up_ref[...]
+    known_ref[4:6, :] = down_ref[...]
+    known_ref[6:8, :] = jnp.zeros_like(down_ref)
+    ids = pltpu.roll(ids_ref[...].astype(jnp.float32), quarter(lax.axis_index("cuts")) * blocks, 1)
     payload_ref[params * blocks :, :] = ids.astype(jnp.bfloat16)
     copies[0].wait()
     for p in range(params):
@@ -81,27 +88,33 @@
     return total
 
 
-def columns(ref, blocks):
-    return [column(ref[i : i + 1, :], blocks) for i in range(ref.shape[0])]
-
-
-def radial_kernel(up_ref, down_ref, all_ref, to_up_ref, to_down_ref):
+def columns(known_ref, late_ref, first, count, blocks):
+    ids = known_ref[first : first + count, :] + late_ref[...]
+    return jnp.concatenate([column(ids[i : i + 1], blocks) for i in range(count)], axis=0)
+
+
+def radial_kernel(known_ref, late_up_ref, late_down_ref, all_ref, to_up_ref, to_down_ref):
     count = to_up_ref.shape[0]
-    blocks = count // up_ref.shape[0]
+    blocks = count // 2
     params = to_up_ref.shape[1] // all_ref.shape[2]
-    wanted = jnp.concatenate(columns(up_ref, blocks) + columns(down_ref, blocks), axis=0)
+    wanted = jnp.concatenate(
+        [columns(known_ref, late_up_ref, 2, 2, blocks), columns(known_ref, late_down_ref, 4, 2, blocks)],
+        axis=0,
+    )
     total = patch_sums(wanted, all_ref, params, blocks).astype(jnp.bfloat16)
     to_up_ref[...] = total[:count]
     to_down_ref[...] = total[count:]
 
 
-def lateral_kernel(offsets_ref, band_ref, radial_ref, wants_ref, all_ref, out_ref):
+def lateral_kernel(offsets_ref, band_ref, radial_ref, known_ref, late_other_ref, all_ref, out_ref):
     width = all_ref.shape[2]
     params, bands = band_ref.shape
     count = out_ref.shape[0] - 8
-    blocks = count // wants_ref.shape[0]
+    blocks = count // 2
     patches = all_ref.shape[0] * 2 * PD
-    mine = jnp.concatenate(columns(wants_ref, blocks), axis=0)
+    mine = jnp.concatenate(
+        [column(known_ref[0:1, :], blocks), columns(known_ref, late_other_ref, 1, 1, blocks)], axis=0
+    )
     wanted = [mine]
     for j in range(bands):
         moved = mine + offsets_ref[j]
@@ -173,17 +186,31 @@
     cuts, rows = lax.axis_size("cuts"), lax.axis_size("group")
     chips = cuts // CORES
     values = params * width
-    partner = [(CORES * z + c, CORES * (z ^ 1) + c) for z in range(chips) for c in range(CORES)]
-    higher = [(i, i + 1) for i in range(rows - 1)]
-    lower = [(j, i) for i, j in higher]
+    axes = ("group", "cuts")
+
+    def permute(value, chosen, rise, flip):
+        pairs = [
+            (r * cuts + CORES * z + c, (r + rise) * cuts + CORES * (z ^ flip) + c)
+            for r in range(max(0, -rise), min(rows, rows - rise))
+            for z in chosen
+            for c in range(CORES)
+        ]
+        return lax.ppermute(value, axes, pairs)
+
+    def wanted_near(own, chosen):
+        other = permute(own, chosen, 0, 1)
+        both = jnp.concatenate([own, other])
+        return other, permute(both, chosen, -1, 0), permute(both, chosen, 1, 0)
+
+    first, last = range(chips // 4), range(chips // 4, chips)
     own = block_owner[:, :, 0] * PD + block_local
-    wants = jnp.concatenate([own, lax.ppermute(own, "cuts", partner)])
-    wants_of_lower = lax.ppermute(wants, "group", higher)
-    wants_of_higher = lax.ppermute(wants, "group", lower)
-    payload = call(
+    payload, known = call(
         project_kernel,
-        [HBM] * 2 + [VMEM] * 2,
-        jax.ShapeDtypeStruct((params * blocks + ID_ROWS, width), jnp.bfloat16),
+        [HBM] * 2 + [VMEM] * 5,
+        (
+            jax.ShapeDtypeStruct((params * blocks + ID_ROWS, width), jnp.bfloat16),
+            jax.ShapeDtypeStruct((8, blocks), jnp.int32),
+        ),
         2 * blocks * params * points * width,
         [
             pltpu.VMEM(gradient.shape, gradient.dtype),
@@ -192,26 +219,33 @@
             pltpu.VMEM((ID_ROWS, 128), jnp.int32),
             pltpu.SemaphoreType.DMA((2,)),
         ],
-    )(gradient, basis, own, valid_count)
+    )(gradient, basis, own, valid_count, *wanted_near(own, first))
     halves = [[CORES * z + c for z in range(h, chips, 2) for c in range(CORES)] for h in range(2)]
     gathered = lax.all_gather(payload, "cuts", axis_index_groups=halves)
+    position = lax.axis_index("cuts")
+    mine = lax.dynamic_slice(
+        gathered,
+        (position // (2 * CORES) * CORES + position % CORES, params * blocks, quarter(position) * blocks),
+        (1, 2, blocks),
+    )[0].astype(jnp.int32)
+    late_other, late_higher, late_lower = wanted_near(mine[0:1] * PD + mine[1:2], last)
     piece = jax.ShapeDtypeStruct((2 * blocks, values), jnp.bfloat16)
     one_hot = blocks * blocks * cuts * values
-    to_higher, to_lower = call(radial_kernel, [VMEM] * 3, (piece, piece), 4 * one_hot)(
-        wants_of_higher, wants_of_lower, gathered
-    )
-    from_lower = lax.ppermute(to_higher, "group", higher)
-    from_higher = lax.ppermute(to_lower, "group", lower)
+    to_higher, to_lower = call(radial_kernel, [VMEM] * 4, (piece, piece), 4 * one_hot)(
+        known, late_higher, late_lower, gathered
+    )
+    from_lower = permute(to_higher, range(chips), 1, 0)
+    from_higher = permute(to_lower, range(chips), -1, 0)
     part = call(
         lateral_kernel,
-        [SMEM] * 3 + [VMEM] * 2,
+        [SMEM] * 3 + [VMEM] * 3,
         jax.ShapeDtypeStruct((2 * blocks + 8, values), jnp.float32),
         10 * one_hot,
-    )(band_offsets, band_weight, radial_weight, wants, gathered)
+    )(band_offsets, band_weight, radial_weight, known, late_other, gathered)
     for_partner = call(
         partner_kernel, [VMEM] * 3, jax.ShapeDtypeStruct((blocks, values), jnp.bfloat16), blocks * values
     )(part, from_lower, from_higher)
-    from_partner = lax.ppermute(for_partner, "cuts", partner)
+    from_partner = permute(for_partner, range(chips), 0, 1)
     return call(
         expand_kernel,
         [VMEM] * 6,

time: 82.5 us -> 88.1 us (1.068)
  the two profiles are of different devices: /device:TPU:22 before, /device:TPU:302 now
where the time goes in v3:
time: 88.1 us; the launch traced here: 87.7 us
  blocking collectives  45.3 us (51%)
  starting transfers between devices  22.4 us (25%)
  waiting for transfers between devices  13.5 us (15%)
  Pallas kernels  3.62 us (4%)
  local copies, waits for them, and re-layouts  1.86 us (2%)
    all_gather x1, blocking collectives, body(): gathered = lax.all_gather(payload, 'cuts', axis_index_groups=halves)  45.3 us
    ppermute x9, starting transfers between devices, permute(): return lax.ppermute(value, axes, pairs)  22.4 us
    ppermute x9, waiting for transfers between devices, permute(): return lax.ppermute(value, axes, pairs)  13.5 us
    unnamed x14, local copies, waits for them, and re-layouts  1.86 us
  transfers between devices with their start and end apart: 9, of which 4 were waited for; matrix products, arithmetic and copies ran while one was open for 0% of the time, Pallas kernels for 1%

profile of v3, /device:TPU:302, one launch (start us, length us, event | category | flops | bytes accessed | tf_op | source)
XLA Modules:
  0.0 87.7 jit_solution(9290708308251572775)
XLA Ops:
  0.0 0.0 copy-start.2
  0.0 0.7 bitcast_add_fusion.patch_ref
  0.7 0.6 collective-permute-start
  1.4 0.0 collective-permute-done.other_ref
  1.4 0.7 collective-permute-start.1
  2.1 0.7 collective-permute-start.2
  2.8 0.0 copy-start.3
  2.8 0.0 collective-permute-done.1.up_ref
  2.8 0.0 collective-permute-done.2.down_ref
  2.8 0.0 copy-done.2
  2.8 0.6 copy-done.3
  3.4 0.0 copy-start
  3.4 1.2 %copy-done = bf16[1,32,128,128]{3,2,1,0:T(8,128)(2,1)S(1)} copy-done((bf16[1,32,128,128]{3,2,1,0:T(8,128)(2,1)S(1)}, bf16[1,32,128,128]{3,2,1,0:T(8,128)(2,1)}, u32[]{:S(2)}) %copy-start) | copy-done | bytes 1048600
  4.6 0.6 shard_map.82
  5.3 0.0 copy-start.4
  5.3 0.0 copy-start.5
  5.3 0.0 copy-start.6
  5.3 45.3 %all-gather = bf16[3328,128]{1,0:T(8,128)(2,1)S(1)} all-gather(bf16[104,128]{1,0:T(8,128)(2,1)S(1)} %get-tuple-element.10), channel_id=2, replica_groups={{0,1,4,5,8,9,12,13,16,17,20,21,24,25,28,29,32,33,36,37,40,41,44,45,48,4..., dimensions={0}, use_global_device_ids=true | all-gather | bytes 878592 | tf_op jit(solution)/shard_map/all_gather | solution.py:224
  50.6 0.0 copy-start.1
  50.6 0.1 dynamic-slice_convert_fusion
  50.7 2.0 %collective-permute-start.3 = (s32[1,32]{1,0:T(1,128)S(1)}, s32[1,32]{1,0:T(1,128)S(1)}, u32[]{:S(2)}, u32[]{:S(2)}) collective-permute-start(s32[1,32]{1,0:T(1,128)S(1)} %add_bitcast_fusion), channel_id=1, source_target_pairs={{16,18},{17,19},{18,16},{19,17},{20,22},{21,23},{22,20},{23,21},{2... | collective-permute-start | bytes 392 | tf_op jit(solution)/shard_map/ppermute | solution.py:198
  52.8 3.5 %collective-permute-done.3.late_other_ref = s32[1,32]{1,0:T(1,128)S(1)} collective-permute-done((s32[1,32]{1,0:T(1,128)S(1)}, s32[1,32]{1,0:T(1,128)S(1)}, u32[]{:S(2)}, u32[]{:S(2)}) %collective-permute-start.3) | collective-permute-done | bytes 160 | tf_op jit(solution)/shard_map/ppermute | solution.py:198
  56.3 1.9 %collective-permute-start.4 = (s32[2,32]{1,0:T(2,128)S(1)}, s32[2,32]{1,0:T(2,128)S(1)}, u32[]{:S(2)}, u32[]{:S(2)}) collective-permute-start(s32[2,32]{1,0:T(2,128)S(1)} %pad_add_fusion.1), channel_id=1, source_target_pairs={{80,16},{81,17},{82,18},{83,19},{84,20},{85,21},{86,22},{87,23},{8... | collective-permute-start | bytes 776 | tf_op jit(solution)/shard_map/ppermute | solution.py:198
  58.2 6.3 %collective-permute-start.5 = (s32[2,32]{1,0:T(2,128)S(1)}, s32[2,32]{1,0:T(2,128)S(1)}, u32[]{:S(2)}, u32[]{:S(2)}) collective-permute-start(s32[2,32]{1,0:T(2,128)S(1)} %pad_add_fusion.1), channel_id=1, source_target_pairs={{16,80},{17,81},{18,82},{19,83},{20,84},{21,85},{22,86},{23,87},{2... | collective-permute-start | bytes 776 | tf_op jit(solution)/shard_map/ppermute | solution.py:198
  64.5 0.0 collective-permute-done.4.late_up_ref
  64.5 1.3 %collective-permute-done.5.late_down_ref = s32[2,32]{1,0:T(2,128)S(1)} collective-permute-done((s32[2,32]{1,0:T(2,128)S(1)}, s32[2,32]{1,0:T(2,128)S(1)}, u32[]{:S(2)}, u32[]{:S(2)}) %collective-permute-start.5) | collective-permute-done | bytes 288 | tf_op jit(solution)/shard_map/ppermute | solution.py:198
  65.8 0.5 shard_map.84
  66.3 6.3 %collective-permute-start.6 = (bf16[64,384]{1,0:T(8,128)(2,1)S(1)}, bf16[64,384]{1,0:T(8,128)(2,1)S(1)}, u32[]{:S(2)}, u32[]{:S(2)}) collective-permute-start(bf16[64,384]{1,0:T(8,128)(2,1)S(1)} %get-tuple-element.11), channel_id=1, source_target_pairs={{0,64},{1,65},{2,66},{3,67},{4,68},{5,69},{6,70},{7,71},{8,72},{9,... | collective-permute-start | bytes 147464 | tf_op jit(solution)/shard_map/ppermute | solution.py:198
  72.6 1.9 %collective-permute-start.7 = (bf16[64,384]{1,0:T(8,128)(2,1)S(1)}, bf16[64,384]{1,0:T(8,128)(2,1)S(1)}, u32[]{:S(2)}, u32[]{:S(2)}) collective-permute-start(bf16[64,384]{1,0:T(8,128)(2,1)S(1)} %get-tuple-element.12), channel_id=1, source_target_pairs={{64,0},{65,1},{66,2},{67,3},{68,4},{69,5},{70,6},{71,7},{72,8},{73... | collective-permute-start | bytes 147464 | tf_op jit(solution)/shard_map/ppermute | solution.py:198
  74.5 0.0 copy-done.4
  74.5 0.0 copy-done.5
  74.5 0.0 copy-done.6
  74.5 1.2 %shard_map.83.part_ref = f32[72,384]{1,0:T(8,128)S(1)} custom-call(s32[4]{0:T(128)S(1)} %copy-done.5, f32[3,4]{1,0:T(4,128)S(1)} %copy-done.4, f32[3]{0:T(128)S(1)} %copy-done.6, s32[8,32]{1,0:T(8,128)S(1)} %get-tuple-element.9.known_ref, s32[1,32]{1,0:T(1,128)S(1)} %collective-permute-done.3.late_other_ref, bf16[32,104,128]{2,1,0:T(8,128)(2,1)S(1)} %bitcast.7), custom_call_target="tpu_custom_call" | custom-call | flops 251658240 | bytes 2097152 | tf_op jit(solution)/shard_map/pallas_call | solution.py:239
  75.8 0.0 collective-permute-done.6.up_ref
  75.8 4.9 %collective-permute-done.7.down_ref = bf16[64,384]{1,0:T(8,128)(2,1)S(1)} collective-permute-done((bf16[64,384]{1,0:T(8,128)(2,1)S(1)}, bf16[64,384]{1,0:T(8,128)(2,1)S(1)}, u32[]{:S(2)}, u32[]{:S(2)}) %collective-permute-start.7) | collective-permute-done | bytes 49184 | tf_op jit(solution)/shard_map/ppermute | solution.py:198
  80.7 1.9 %collective-permute-start.8 = (bf16[32,384]{1,0:T(8,128)(2,1)S(1)}, bf16[32,384]{1,0:T(8,128)(2,1)S(1)}, u32[]{:S(2)}, u32[]{:S(2)}) collective-permute-start(bf16[32,384]{1,0:T(8,128)(2,1)S(1)} %shard_map.85), channel_id=1, source_target_pairs={{0,2},{1,3},{2,0},{3,1},{4,6},{5,7},{6,4},{7,5},{8,10},{9,11},{10,... | collective-permute-start | bytes 73736 | tf_op jit(solution)/shard_map/ppermute | solution.py:198
  82.6 3.8 %collective-permute-done.8.other_ref = bf16[32,384]{1,0:T(8,128)(2,1)S(1)} collective-permute-done((bf16[32,384]{1,0:T(8,128)(2,1)S(1)}, bf16[32,384]{1,0:T(8,128)(2,1)S(1)}, u32[]{:S(2)}, u32[]{:S(2)}) %collective-permute-start.8) | collective-permute-done | bytes 24608 | tf_op jit(solution)/shard_map/ppermute | solution.py:198
  86.4 0.0 copy-done.1
  86.4 1.3 %shard_map.86 = f32[3,1,32,128]{3,2,1,0:T(8,128)} custom-call(f32[72,384]{1,0:T(8,128)S(1)} %shard_map.83.part_ref, bf16[64,384]{1,0:T(8,128)(2,1)S(1)} %collective-permute-done.6.up_ref, bf16[64,384]{1,0:T(8,128)(2,1)S(1)} %collective-permute-done.7.down_ref, bf16[32,384]{1,0:T(8,128)(2,1)S(1)} %collective-permute-done.8.other_ref, ...), custom_call_target="tpu_custom_call" | custom-call | flops 3145728 | bytes 2097152 | tf_op jit(solution)/shard_map/pallas_call | solution.py:249
  (4 shorter events, 0.0 us)
Async XLA Ops:
  0.0 2.8 %copy-start.2 = (f32[3,1,32,128]{3,2,1,0:T(8,128)S(1)}, f32[3,1,32,128]{3,2,1,0:T(8,128)}, u32[]{:S(2)}) copy-start(f32[3,1,32,128]{3,2,1,0:T(8,128)} %gradient_hbm.1) | copy-start | bytes 147460
  0.7 0.7 collective-permute-start
  1.4 1.4 %collective-permute-start.1 = (s32[2,32]{1,0:T(2,128)S(1)}, s32[2,32]{1,0:T(2,128)S(1)}, u32[]{:S(2)}, u32[]{:S(2)}) collective-permute-start(s32[2,32]{1,0:T(2,128)S(1)} %pad_add_fusion), channel_id=1, source_target_pairs={{64,0},{65,1},{66,2},{67,3},{68,4},{69,5},{70,6},{71,7},{72,8},{73... | collective-permute-start | bytes 776 | tf_op jit(solution)/shard_map/ppermute | solution.py:198
  2.1 0.7 collective-permute-start.2
  2.8 0.7 copy-start.3
  3.4 1.2 %copy-start = (bf16[1,32,128,128]{3,2,1,0:T(8,128)(2,1)S(1)}, bf16[1,32,128,128]{3,2,1,0:T(8,128)(2,1)}, u32[]{:S(2)}) copy-start(bf16[1,32,128,128]{3,2,1,0:T(8,128)(2,1)} %basis_ref.1) | copy-start | bytes 3145732
  5.3 69.2 %copy-start.4 = (f32[3,4]{1,0:T(4,128)S(1)}, f32[3,4]{1,0:T(4,128)}, u32[]{:S(2)}) copy-start(f32[3,4]{1,0:T(4,128)} %band_ref.1) | copy-start | bytes 148
  5.3 69.2 %copy-start.5 = (s32[4]{0:T(128)S(1)}, s32[4]{0:T(128)}, u32[]{:S(2)}) copy-start(s32[4]{0:T(128)} %offsets_ref.1) | copy-start | bytes 52
  5.3 69.2 %copy-start.6 = (f32[3]{0:T(128)S(1)}, f32[3]{0:T(128)}, u32[]{:S(2)}) copy-start(f32[3]{0:T(128)} %radial_ref.1) | copy-start | bytes 40
  50.6 35.8 %copy-start.1 = (bf16[1,32,128,128]{3,2,1,0:T(8,128)(2,1)S(1)}, bf16[1,32,128,128]{3,2,1,0:T(8,128)(2,1)}, u32[]{:S(2)}) copy-start(bf16[1,32,128,128]{3,2,1,0:T(8,128)(2,1)} %basis_ref.1) | copy-start | bytes 3145732
  50.7 5.6 %collective-permute-start.3 = (s32[1,32]{1,0:T(1,128)S(1)}, s32[1,32]{1,0:T(1,128)S(1)}, u32[]{:S(2)}, u32[]{:S(2)}) collective-permute-start(s32[1,32]{1,0:T(1,128)S(1)} %add_bitcast_fusion), channel_id=1, source_target_pairs={{16,18},{17,19},{18,16},{19,17},{20,22},{21,23},{22,20},{23,21},{2... | collective-permute-start | bytes 392 | tf_op jit(solution)/shard_map/ppermute | solution.py:198
  56.3 8.2 %collective-permute-start.4 = (s32[2,32]{1,0:T(2,128)S(1)}, s32[2,32]{1,0:T(2,128)S(1)}, u32[]{:S(2)}, u32[]{:S(2)}) collective-permute-start(s32[2,32]{1,0:T(2,128)S(1)} %pad_add_fusion.1), channel_id=1, source_target_pairs={{80,16},{81,17},{82,18},{83,19},{84,20},{85,21},{86,22},{87,23},{8... | collective-permute-start | bytes 776 | tf_op jit(solution)/shard_map/ppermute | solution.py:198
  58.2 7.6 %collective-permute-start.5 = (s32[2,32]{1,0:T(2,128)S(1)}, s32[2,32]{1,0:T(2,128)S(1)}, u32[]{:S(2)}, u32[]{:S(2)}) collective-permute-start(s32[2,32]{1,0:T(2,128)S(1)} %pad_add_fusion.1), channel_id=1, source_target_pairs={{16,80},{17,81},{18,82},{19,83},{20,84},{21,85},{22,86},{23,87},{2... | collective-permute-start | bytes 776 | tf_op jit(solution)/shard_map/ppermute | solution.py:198
  66.3 9.5 %collective-permute-start.6 = (bf16[64,384]{1,0:T(8,128)(2,1)S(1)}, bf16[64,384]{1,0:T(8,128)(2,1)S(1)}, u32[]{:S(2)}, u32[]{:S(2)}) collective-permute-start(bf16[64,384]{1,0:T(8,128)(2,1)S(1)} %get-tuple-element.11), channel_id=1, source_target_pairs={{0,64},{1,65},{2,66},{3,67},{4,68},{5,69},{6,70},{7,71},{8,72},{9,... | collective-permute-start | bytes 147464 | tf_op jit(solution)/shard_map/ppermute | solution.py:198
  72.6 8.1 %collective-permute-start.7 = (bf16[64,384]{1,0:T(8,128)(2,1)S(1)}, bf16[64,384]{1,0:T(8,128)(2,1)S(1)}, u32[]{:S(2)}, u32[]{:S(2)}) collective-permute-start(bf16[64,384]{1,0:T(8,128)(2,1)S(1)} %get-tuple-element.12), channel_id=1, source_target_pairs={{64,0},{65,1},{66,2},{67,3},{68,4},{69,5},{70,6},{71,7},{72,8},{73... | collective-permute-start | bytes 147464 | tf_op jit(solution)/shard_map/ppermute | solution.py:198
  80.7 5.7 %collective-permute-start.8 = (bf16[32,384]{1,0:T(8,128)(2,1)S(1)}, bf16[32,384]{1,0:T(8,128)(2,1)S(1)}, u32[]{:S(2)}, u32[]{:S(2)}) collective-permute-start(bf16[32,384]{1,0:T(8,128)(2,1)S(1)} %shard_map.85), channel_id=1, source_target_pairs={{0,2},{1,3},{2,0},{3,1},{4,6},{5,7},{6,4},{7,5},{8,10},{9,11},{10,... | collective-permute-start | bytes 73736 | tf_op jit(solution)/shard_map/ppermute | solution.py:198

commit v4 on v2

--- a/solution.py
+++ b/solution.py
@@ -7,6 +7,7 @@
 
 PD = 16
 CORES = 2
+NEAR = 4
 ID_ROWS = 8
 
 
@@ -36,10 +37,10 @@
     params, _, blocks, points = gradient_ref.shape
     inside = inside_mask(valid_ref, blocks, points)
     ids_ref[...] = jnp.zeros_like(ids_ref)
-    ids_ref[0:1, 0:blocks] = patch_ref[...] // PD
-    ids_ref[1:2, 0:blocks] = patch_ref[...] % PD
+    ids_ref[0:1, 0:blocks] = patch_ref[0:1, :] // PD
+    ids_ref[1:2, 0:blocks] = patch_ref[0:1, :] % PD
     position = lax.axis_index("cuts")
-    quarter = (position // (2 * CORES)) % 2 * CORES + position % CORES
+    quarter = (position // (NEAR * CORES)) % 2 * CORES + position % CORES
     ids = pltpu.roll(ids_ref[...].astype(jnp.float32), quarter * blocks, 1)
     payload_ref[params * blocks :, :] = ids.astype(jnp.bfloat16)
     copies[0].wait()
@@ -95,12 +96,14 @@
     to_down_ref[...] = total[count:]
 
 
-def lateral_kernel(offsets_ref, band_ref, radial_ref, wants_ref, all_ref, out_ref):
+def lateral_kernel(offsets_ref, band_ref, radial_ref, wants_ref, all_ref, basis_ref, out_ref, turned_ref):
+    for b in range(turned_ref.shape[0]):
+        turned_ref[b] = basis_ref[0, b].T
     width = all_ref.shape[2]
     params, bands = band_ref.shape
     count = out_ref.shape[0] - 8
-    blocks = count // wants_ref.shape[0]
-    patches = all_ref.shape[0] * 2 * PD
+    blocks = count // NEAR
+    patches = all_ref.shape[0] * NEAR * PD
     mine = jnp.concatenate(columns(wants_ref, blocks), axis=0)
     wanted = [mine]
     for j in range(bands):
@@ -119,29 +122,24 @@
         out_ref[count:, p * width : (p + 1) * width] = jnp.full((8, width), radial_ref[p], jnp.float32)
 
 
-def radial_added(part_ref, up_ref, down_ref, first, blocks):
+def near_kernel(part_ref, up_ref, down_ref, out_ref):
+    _, blocks, _ = out_ref.shape
     count = up_ref.shape[0]
-    rows = slice(first, first + blocks)
-    neighbours = up_ref[rows, :].astype(jnp.float32) + down_ref[rows, :].astype(jnp.float32)
-    return part_ref[rows, :] + part_ref[count : count + 1, :] * neighbours
-
-
-def partner_kernel(part_ref, up_ref, down_ref, out_ref):
-    blocks = out_ref.shape[0]
-    out_ref[...] = radial_added(part_ref, up_ref, down_ref, blocks, blocks).astype(out_ref.dtype)
-
-
-def expand_kernel(part_ref, up_ref, down_ref, other_ref, basis_ref, valid_ref, out_ref, rows_ref):
+    for i in range(NEAR):
+        rows = slice(i * blocks, (i + 1) * blocks)
+        neighbours = up_ref[rows, :].astype(jnp.float32) + down_ref[rows, :].astype(jnp.float32)
+        out_ref[i] = (part_ref[rows, :] + part_ref[count : count + 1, :] * neighbours).astype(out_ref.dtype)
+
+
+def expand_kernel(parts_ref, turned_ref, valid_ref, out_ref, rows_ref):
     params, _, blocks, points = out_ref.shape
-    width = basis_ref.shape[3]
-    smooth = radial_added(part_ref, up_ref, down_ref, 0, blocks) + other_ref[...].astype(jnp.float32)
+    width = turned_ref.shape[1]
+    smooth = sum(parts_ref[i].astype(jnp.float32) for i in range(NEAR))
     for p in range(params):
         rows_ref[p] = smooth[:, p * width : (p + 1) * width]
     for b in range(blocks):
         picked = rows_ref[:, b, :].astype(jnp.bfloat16)
-        rows_ref[:, b, :] = lax.dot_general(
-            picked, basis_ref[0, b], (((1,), (1,)), ((), ())), preferred_element_type=jnp.float32
-        )
+        rows_ref[:, b, :] = jnp.dot(picked, turned_ref[b], preferred_element_type=jnp.float32)
     inside = inside_mask(valid_ref, blocks, points)
     for p in range(params):
         out_ref[p, 0] = jnp.where(inside, rows_ref[p], 0.0)
@@ -173,11 +171,16 @@
     cuts, rows = lax.axis_size("cuts"), lax.axis_size("group")
     chips = cuts // CORES
     values = params * width
-    partner = [(CORES * z + c, CORES * (z ^ 1) + c) for z in range(chips) for c in range(CORES)]
+    sets = [
+        [CORES * (first + i) + c for i in range(NEAR)]
+        for first in range(0, chips, NEAR)
+        for c in range(CORES)
+    ]
     higher = [(i, i + 1) for i in range(rows - 1)]
     lower = [(j, i) for i, j in higher]
-    own = block_owner[:, :, 0] * PD + block_local
-    wants = jnp.concatenate([own, lax.ppermute(own, "cuts", partner)])
+    copies = (NEAR, blocks)
+    own = jnp.broadcast_to(block_owner[:, :, 0], copies) * PD + jnp.broadcast_to(block_local, copies)
+    wants = lax.all_to_all(own, "cuts", 0, 0, axis_index_groups=sets, tiled=True)
     wants_of_lower = lax.ppermute(wants, "group", higher)
     wants_of_higher = lax.ppermute(wants, "group", lower)
     payload = call(
@@ -193,32 +196,40 @@
             pltpu.SemaphoreType.DMA((2,)),
         ],
     )(gradient, basis, own, valid_count)
-    halves = [[CORES * z + c for z in range(h, chips, 2) for c in range(CORES)] for h in range(2)]
-    gathered = lax.all_gather(payload, "cuts", axis_index_groups=halves)
-    piece = jax.ShapeDtypeStruct((2 * blocks, values), jnp.bfloat16)
+    shares = [
+        [CORES * z + c for z in range(first, chips, NEAR) for c in range(CORES)] for first in range(NEAR)
+    ]
+    gathered = lax.all_gather(payload, "cuts", axis_index_groups=shares)
+    piece = jax.ShapeDtypeStruct((NEAR * blocks, values), jnp.bfloat16)
     one_hot = blocks * blocks * cuts * values
     to_higher, to_lower = call(radial_kernel, [VMEM] * 3, (piece, piece), 4 * one_hot)(
         wants_of_higher, wants_of_lower, gathered
     )
     from_lower = lax.ppermute(to_higher, "group", higher)
     from_higher = lax.ppermute(to_lower, "group", lower)
-    part = call(
+    part, turned = call(
         lateral_kernel,
-        [SMEM] * 3 + [VMEM] * 2,
-        jax.ShapeDtypeStruct((2 * blocks + 8, values), jnp.float32),
+        [SMEM] * 3 + [VMEM] * 3,
+        (
+            jax.ShapeDtypeStruct((NEAR * blocks + 8, values), jnp.float32),
+            jax.ShapeDtypeStruct((blocks, width, points), basis.dtype),
+        ),
         10 * one_hot,
-    )(band_offsets, band_weight, radial_weight, wants, gathered)
-    for_partner = call(
-        partner_kernel, [VMEM] * 3, jax.ShapeDtypeStruct((blocks, values), jnp.bfloat16), blocks * values
+    )(band_offsets, band_weight, radial_weight, wants, gathered, basis)
+    for_near = call(
+        near_kernel,
+        [VMEM] * 3,
+        jax.ShapeDtypeStruct((NEAR, blocks, values), jnp.bfloat16),
+        NEAR * blocks * values,
     )(part, from_lower, from_higher)
-    from_partner = lax.ppermute(for_partner, "cuts", partner)
+    parts = lax.all_to_all(for_near, "cuts", 0, 0, axis_index_groups=sets, tiled=True)
     return call(
         expand_kernel,
-        [VMEM] * 6,
+        [VMEM] * 3,
         jax.ShapeDtypeStruct((params, 1, blocks, points), jnp.float32),
         2 * blocks * params * points * width,
         [pltpu.VMEM((params, blocks, width), jnp.float32)],
-    )(part, from_lower, from_higher, from_partner, basis, valid_count)
+    )(parts, turned, valid_count)
 
 
 def solution(mesh):

time: 82.5 us -> 81.4 us (0.987)
  the two profiles are of different devices: /device:TPU:22 before, /device:TPU:14 now
where the time goes in v4:
time: 81.4 us; the launch traced here: 81 us
  blocking collectives  46.4 us (57%)
  starting transfers between devices  19.3 us (24%)
  waiting for transfers between devices  7.7 us (9%)
  Pallas kernels  3.46 us (4%)
  local copies, waits for them, and re-layouts  3.28 us (4%)
    all_gather x1, blocking collectives, body(): gathered = lax.all_gather(payload, 'cuts', axis_index_groups=shares)  38 us
    all_to_all x1, blocking collectives, body(): lax.all_to_all(for_near, 'cuts', 0, 0, axis_index_groups=sets, tiled=True)  8.42 us
    all_to_all x1, starting transfers between devices, body(): lax.all_to_all(own, 'cuts', 0, 0, axis_index_groups=sets, tiled=True)  5.89 us
    ppermute x1, starting transfers between devices, body(): from_lower = lax.ppermute(to_higher, 'group', higher)  5.64 us
    ppermute x1, waiting for transfers between devices, body(): from_higher = lax.ppermute(to_lower, 'group', lower)  5.53 us
    ppermute x1, starting transfers between devices, body(): wants_of_lower = lax.ppermute(wants, 'group', higher)  3.39 us
    unnamed x14, local copies, waits for them, and re-layouts  2.7 us
    ppermute x1, starting transfers between devices, body(): wants_of_higher = lax.ppermute(wants, 'group', lower)  2.44 us
  transfers between devices with their start and end apart: 5, of which 2 were waited for; matrix products, arithmetic and copies ran while one was open for 0% of the time, Pallas kernels for 2%

profile of v4, /device:TPU:14, one launch (start us, length us, event | category | flops | bytes accessed | tf_op | source)
XLA Modules:
  0.0 81.0 jit_solution(12125325644936652258)
XLA Ops:
  0.0 0.7 bitcast_add_fusion
  0.7 0.6 broadcast_in_dim.13
  1.3 5.9 %all-to-all-start = ((s32[4,1,32]{2,1,0:T(1,128)}), s32[4,1,32]{2,1,0:T(1,128)S(1)}, u32[]{:S(2)}, u32[]{:S(2)}) async-start(s32[4,1,32]{2,1,0:T(1,128)} %broadcast_in_dim.13), calls=%async_computation | async-start | bytes 4096 | tf_op jit(solution)/shard_map/all_to_all | solution.py:183
  7.2 0.0 copy-start.4
  7.2 0.7 copy-done.4
  7.8 0.0 copy-start
  7.8 1.2 %copy-done = bf16[1,32,128,128]{3,2,1,0:T(8,128)(2,1)S(1)} copy-done((bf16[1,32,128,128]{3,2,1,0:T(8,128)(2,1)S(1)}, bf16[1,32,128,128]{3,2,1,0:T(8,128)(2,1)}, u32[]{:S(2)}) %copy-start) | copy-done | bytes 1048600
  9.0 0.0 copy-start.2
  9.0 0.8 copy-done.2
  9.8 0.0 copy-start.1
  9.8 0.6 shard_map.82
  10.5 2.2 %all-to-all-done = s32[4,1,32]{2,1,0:T(1,128)S(1)} async-done(((s32[4,1,32]{2,1,0:T(1,128)}), s32[4,1,32]{2,1,0:T(1,128)S(1)}, u32[]{:S(2)}, u32[]{:S(2)}) %all-to-all-start) | async-done | bytes 544 | tf_op jit(solution)/shard_map/all_to_all | solution.py:183
  12.6 3.4 %collective-permute-start.1 = (s32[4,32]{1,0:T(4,128)S(1)}, s32[4,32]{1,0:T(4,128)S(1)}, u32[]{:S(2)}, u32[]{:S(2)}) collective-permute-start(s32[4,32]{1,0:T(4,128)S(1)} %bitcast.8), channel_id=1, source_target_pairs={{0,64},{64,128},{128,192},{192,256},{256,320},{320,384},{384,448},... | collective-permute-start | bytes 1544 | tf_op jit(solution)/shard_map/ppermute | solution.py:184
  16.0 2.4 %collective-permute-start = (s32[4,32]{1,0:T(4,128)S(1)}, s32[4,32]{1,0:T(4,128)S(1)}, u32[]{:S(2)}, u32[]{:S(2)}) collective-permute-start(s32[4,32]{1,0:T(4,128)S(1)} %bitcast.9), channel_id=1, source_target_pairs={{64,0},{128,64},{192,128},{256,192},{320,256},{384,320},{448,384},... | collective-permute-start | bytes 1544 | tf_op jit(solution)/shard_map/ppermute | solution.py:185
  18.5 38.0 %all-gather = bf16[1664,128]{1,0:T(8,128)(2,1)S(1)} all-gather(bf16[104,128]{1,0:T(8,128)(2,1)S(1)} %shard_map.82), channel_id=2, replica_groups={{0,1,8,9,16,17,24,25,32,33,40,41,48,49,56,57},{2,3,10,11,18,19,26,27,34..., dimensions={0}, use_global_device_ids=true | all-gather | bytes 452608 | tf_op jit(solution)/shard_map/all_gather | solution.py:202
  56.5 0.0 collective-permute-done.1.down_ref
  56.5 0.0 collective-permute-done.up_ref
  56.5 0.5 shard_map.84
  57.0 0.0 copy-start.3
  57.0 0.0 copy-start.5
  57.0 0.0 copy-start.6
  57.0 5.6 %collective-permute-start.2 = (bf16[128,384]{1,0:T(8,128)(2,1)S(1)}, bf16[128,384]{1,0:T(8,128)(2,1)S(1)}, u32[]{:S(2)}, u32[]{:S(2)}) collective-permute-start(bf16[128,384]{1,0:T(8,128)(2,1)S(1)} %get-tuple-element.10), channel_id=1, source_target_pairs={{0,64},{64,128},{128,192},{192,256},{256,320},{320,384},{384,448},... | collective-permute-start | bytes 294920 | tf_op jit(solution)/shard_map/ppermute | solution.py:208
  62.7 1.9 %collective-permute-start.3 = (bf16[128,384]{1,0:T(8,128)(2,1)S(1)}, bf16[128,384]{1,0:T(8,128)(2,1)S(1)}, u32[]{:S(2)}, u32[]{:S(2)}) collective-permute-start(bf16[128,384]{1,0:T(8,128)(2,1)S(1)} %get-tuple-element.11), channel_id=1, source_target_pairs={{64,0},{128,64},{192,128},{256,192},{320,256},{384,320},{448,384},... | collective-permute-start | bytes 294920 | tf_op jit(solution)/shard_map/ppermute | solution.py:209
  64.6 0.0 copy-done.1
  64.6 0.0 copy-done.3
  64.6 0.0 copy-done.5
  64.7 0.0 copy-done.6
  64.7 1.3 %shard_map.83 = (f32[136,384]{1,0:T(8,128)S(1)}, bf16[32,128,128]{2,1,0:T(8,128)(2,1)S(1)}) custom-call(s32[4]{0:T(128)S(1)} %copy-done.5, f32[3,4]{1,0:T(4,128)S(1)} %copy-done.3, f32[3]{0:T(128)S(1)} %copy-done.6, s32[4,32]{1,0:T(4,128)S(1)} %bitcast.10, bf16[16,104,128]{2,1,0:T(8,128)(2,1)S(1)} %bitcast.7, bf16[1,32,128,128]{3,2,1,0:T(8,128)(2,1)S(1)} %copy-done.1), custom_call_target="tpu_custom_call" | custom-call | flops 251658240 | bytes 2097152 | tf_op jit(solution)/shard_map/pallas_call | solution.py:210
  65.9 0.0 collective-permute-done.2.up_ref
  65.9 5.5 %collective-permute-done.3.down_ref = bf16[128,384]{1,0:T(8,128)(2,1)S(1)} collective-permute-done((bf16[128,384]{1,0:T(8,128)(2,1)S(1)}, bf16[128,384]{1,0:T(8,128)(2,1)S(1)}, u32[]{:S(2)}, u32[]{:S(2)}) %collective-permute-start.3) | collective-permute-done | bytes 98336 | tf_op jit(solution)/shard_map/ppermute | solution.py:209
  71.5 8.4 %all_to_all.13.parts_ref = bf16[4,32,384]{2,1,0:T(8,128)(2,1)S(1)} all-to-all(bf16[4,32,384]{2,1,0:T(8,128)(2,1)S(1)} %shard_map.85), channel_id=1, replica_groups={{0,2,4,6},{1,3,5,7},{8,10,12,14},{9,11,13,15},{16,18,20,22},{17,19,21,2..., dimensions={0} | all-to-all | bytes 196608 | tf_op jit(solution)/shard_map/all_to_all | solution.py:225
  79.9 1.0 %shard_map.86 = f32[3,1,32,128]{3,2,1,0:T(8,128)} custom-call(bf16[4,32,384]{2,1,0:T(8,128)(2,1)S(1)} %all_to_all.13.parts_ref, bf16[32,128,128]{2,1,0:T(8,128)(2,1)S(1)} %get-tuple-element.12.turned_ref, s32[1,32]{1,0:T(1,128)S(1)} %copy-done.4), custom_call_target="tpu_custom_call" | custom-call | flops 3145728 | bytes 2097152 | tf_op jit(solution)/shard_map/pallas_call | solution.py:226
  (2 shorter events, 0.0 us)
Async XLA Ops:
  1.3 11.4 %all-to-all-start = ((s32[4,1,32]{2,1,0:T(1,128)}), s32[4,1,32]{2,1,0:T(1,128)S(1)}, u32[]{:S(2)}, u32[]{:S(2)}) async-start(s32[4,1,32]{2,1,0:T(1,128)} %broadcast_in_dim.13), calls=%async_computation | async-start | bytes 4096 | tf_op jit(solution)/shard_map/all_to_all | solution.py:183
  7.2 0.7 copy-start.4
  7.8 1.2 %copy-start = (bf16[1,32,128,128]{3,2,1,0:T(8,128)(2,1)S(1)}, bf16[1,32,128,128]{3,2,1,0:T(8,128)(2,1)}, u32[]{:S(2)}) copy-start(bf16[1,32,128,128]{3,2,1,0:T(8,128)(2,1)} %basis_ref.1) | copy-start | bytes 3145732
  9.0 0.8 copy-start.2
  9.8 54.8 %copy-start.1 = (bf16[1,32,128,128]{3,2,1,0:T(8,128)(2,1)S(1)}, bf16[1,32,128,128]{3,2,1,0:T(8,128)(2,1)}, u32[]{:S(2)}) copy-start(bf16[1,32,128,128]{3,2,1,0:T(8,128)(2,1)} %basis_ref.1) | copy-start | bytes 3145732
  12.6 43.9 %collective-permute-start.1 = (s32[4,32]{1,0:T(4,128)S(1)}, s32[4,32]{1,0:T(4,128)S(1)}, u32[]{:S(2)}, u32[]{:S(2)}) collective-permute-start(s32[4,32]{1,0:T(4,128)S(1)} %bitcast.8), channel_id=1, source_target_pairs={{0,64},{64,128},{128,192},{192,256},{256,320},{320,384},{384,448},... | collective-permute-start | bytes 1544 | tf_op jit(solution)/shard_map/ppermute | solution.py:184
  16.0 40.5 %collective-permute-start = (s32[4,32]{1,0:T(4,128)S(1)}, s32[4,32]{1,0:T(4,128)S(1)}, u32[]{:S(2)}, u32[]{:S(2)}) collective-permute-start(s32[4,32]{1,0:T(4,128)S(1)} %bitcast.9), channel_id=1, source_target_pairs={{64,0},{128,64},{192,128},{256,192},{320,256},{384,320},{448,384},... | collective-permute-start | bytes 1544 | tf_op jit(solution)/shard_map/ppermute | solution.py:185
  57.0 7.6 %copy-start.3 = (f32[3,4]{1,0:T(4,128)S(1)}, f32[3,4]{1,0:T(4,128)}, u32[]{:S(2)}) copy-start(f32[3,4]{1,0:T(4,128)} %band_ref.1) | copy-start | bytes 148
  57.0 7.6 %copy-start.5 = (s32[4]{0:T(128)S(1)}, s32[4]{0:T(128)}, u32[]{:S(2)}) copy-start(s32[4]{0:T(128)} %offsets_ref.1) | copy-start | bytes 52
  57.0 7.6 %copy-start.6 = (f32[3]{0:T(128)S(1)}, f32[3]{0:T(128)}, u32[]{:S(2)}) copy-start(f32[3]{0:T(128)} %radial_ref.1) | copy-start | bytes 40
  57.0 8.9 %collective-permute-start.2 = (bf16[128,384]{1,0:T(8,128)(2,1)S(1)}, bf16[128,384]{1,0:T(8,128)(2,1)S(1)}, u32[]{:S(2)}, u32[]{:S(2)}) collective-permute-start(bf16[128,384]{1,0:T(8,128)(2,1)S(1)} %get-tuple-element.10), channel_id=1, source_target_pairs={{0,64},{64,128},{128,192},{192,256},{256,320},{320,384},{384,448},... | collective-permute-start | bytes 294920 | tf_op jit(solution)/shard_map/ppermute | solution.py:208
  62.7 8.8 %collective-permute-start.3 = (bf16[128,384]{1,0:T(8,128)(2,1)S(1)}, bf16[128,384]{1,0:T(8,128)(2,1)S(1)}, u32[]{:S(2)}, u32[]{:S(2)}) collective-permute-start(bf16[128,384]{1,0:T(8,128)(2,1)S(1)} %get-tuple-element.11), channel_id=1, source_target_pairs={{64,0},{128,64},{192,128},{256,192},{320,256},{384,320},{448,384},... | collective-permute-start | bytes 294920 | tf_op jit(solution)/shard_map/ppermute | solution.py:209

commit v5 on v4

--- a/solution.py
+++ b/solution.py
@@ -82,59 +82,55 @@
     return total
 
 
-def columns(ref, blocks):
-    return [column(ref[i : i + 1, :], blocks) for i in range(ref.shape[0])]
-
-
-def radial_kernel(up_ref, down_ref, all_ref, to_up_ref, to_down_ref):
-    count = to_up_ref.shape[0]
-    blocks = count // up_ref.shape[0]
-    params = to_up_ref.shape[1] // all_ref.shape[2]
-    wanted = jnp.concatenate(columns(up_ref, blocks) + columns(down_ref, blocks), axis=0)
-    total = patch_sums(wanted, all_ref, params, blocks).astype(jnp.bfloat16)
-    to_up_ref[...] = total[:count]
-    to_down_ref[...] = total[count:]
-
-
-def lateral_kernel(offsets_ref, band_ref, radial_ref, wants_ref, all_ref, basis_ref, out_ref, turned_ref):
+def same_core():
+    core = lax.axis_index("cuts") % CORES
+    return [CORES * i + core for i in range(NEAR)]
+
+
+def sums_kernel(
+    offsets_ref, band_ref, radial_ref, wants_ref, all_ref, row_ref, basis_ref, out_ref, turned_ref
+):
     for b in range(turned_ref.shape[0]):
         turned_ref[b] = basis_ref[0, b].T
     width = all_ref.shape[2]
     params, bands = band_ref.shape
-    count = out_ref.shape[0] - 8
-    blocks = count // NEAR
+    near, blocks, _ = out_ref.shape
+    count = NEAR * blocks
     patches = all_ref.shape[0] * NEAR * PD
-    mine = jnp.concatenate(columns(wants_ref, blocks), axis=0)
+    wanted = jnp.concatenate([column(wants_ref[i : i + 1, :], blocks) for i in range(near)], axis=0)
+    beside = patch_sums(wanted, row_ref, params, blocks)
+    for p in range(params):
+        lanes = slice(p * width, (p + 1) * width)
+        radial = beside[:, lanes] * radial_ref[p]
+        for i in range(near):
+            out_ref[i, :, lanes] = radial[i * blocks : (i + 1) * blocks].astype(out_ref.dtype)
+    mine = jnp.concatenate([column(wants_ref[pl.ds(i, 1), :], blocks) for i in same_core()], axis=0)
     wanted = [mine]
     for j in range(bands):
         moved = mine + offsets_ref[j]
         moved = jnp.where(moved < 0, moved + patches, moved)
         wanted.append(jnp.where(moved >= patches, moved - patches, moved))
     total = patch_sums(jnp.concatenate(wanted, axis=0), all_ref, params, blocks)
-    for p in range(params):
-        part = total[:, p * width : (p + 1) * width]
+    core = lax.axis_index("cuts") % CORES
+    for p in range(params):
+        lanes = slice(p * width, (p + 1) * width)
+        part = total[:, lanes]
         centre = part[:count]
         smooth = centre - (2.0 * radial_ref[p]) * centre
         for j in range(bands):
             shifted = part[(j + 1) * count : (j + 2) * count]
             smooth = smooth + band_ref[p, j] * (shifted - centre)
-        out_ref[:count, p * width : (p + 1) * width] = smooth
-        out_ref[count:, p * width : (p + 1) * width] = jnp.full((8, width), radial_ref[p], jnp.float32)
-
-
-def near_kernel(part_ref, up_ref, down_ref, out_ref):
-    _, blocks, _ = out_ref.shape
-    count = up_ref.shape[0]
-    for i in range(NEAR):
-        rows = slice(i * blocks, (i + 1) * blocks)
-        neighbours = up_ref[rows, :].astype(jnp.float32) + down_ref[rows, :].astype(jnp.float32)
-        out_ref[i] = (part_ref[rows, :] + part_ref[count : count + 1, :] * neighbours).astype(out_ref.dtype)
+        radial = beside[:, lanes] * radial_ref[p]
+        for i in range(NEAR):
+            both = [radial[(CORES * i + c) * blocks : (CORES * i + c + 1) * blocks] for c in range(CORES)]
+            added = jnp.where(core == 0, both[0], both[1]) + smooth[i * blocks : (i + 1) * blocks]
+            out_ref[pl.ds(CORES * i + core, 1), :, lanes] = added[None].astype(out_ref.dtype)
 
 
 def expand_kernel(parts_ref, turned_ref, valid_ref, out_ref, rows_ref):
     params, _, blocks, points = out_ref.shape
     width = turned_ref.shape[1]
-    smooth = sum(parts_ref[i].astype(jnp.float32) for i in range(NEAR))
+    smooth = sum(parts_ref[i].astype(jnp.float32) for i in range(parts_ref.shape[0]))
     for p in range(params):
         rows_ref[p] = smooth[:, p * width : (p + 1) * width]
     for b in range(blocks):
@@ -171,18 +167,10 @@
     cuts, rows = lax.axis_size("cuts"), lax.axis_size("group")
     chips = cuts // CORES
     values = params * width
-    sets = [
-        [CORES * (first + i) + c for i in range(NEAR)]
-        for first in range(0, chips, NEAR)
-        for c in range(CORES)
-    ]
-    higher = [(i, i + 1) for i in range(rows - 1)]
-    lower = [(j, i) for i, j in higher]
-    copies = (NEAR, blocks)
-    own = jnp.broadcast_to(block_owner[:, :, 0], copies) * PD + jnp.broadcast_to(block_local, copies)
-    wants = lax.all_to_all(own, "cuts", 0, 0, axis_index_groups=sets, tiled=True)
-    wants_of_lower = lax.ppermute(wants, "group", higher)
-    wants_of_higher = lax.ppermute(wants, "group", lower)
+    near = NEAR * CORES
+    sets = [list(range(first, first + near)) for first in range(0, cuts, near)]
+    own = block_owner[:, :, 0] * PD + block_local
+    wants = lax.all_gather(own, "cuts", axis_index_groups=sets, tiled=True)
     payload = call(
         project_kernel,
         [HBM] * 2 + [VMEM] * 2,
@@ -200,28 +188,24 @@
         [CORES * z + c for z in range(first, chips, NEAR) for c in range(CORES)] for first in range(NEAR)
     ]
     gathered = lax.all_gather(payload, "cuts", axis_index_groups=shares)
-    piece = jax.ShapeDtypeStruct((NEAR * blocks, values), jnp.bfloat16)
+    pairs = [
+        (r * cuts + d, q * cuts + d)
+        for r in range(rows)
+        for d in range(cuts)
+        for q in [r + 1 if d % CORES else r - 1]
+        if 0 <= q < rows
+    ]
+    neighbour = lax.ppermute(gathered, ("group", "cuts"), pairs)
     one_hot = blocks * blocks * cuts * values
-    to_higher, to_lower = call(radial_kernel, [VMEM] * 3, (piece, piece), 4 * one_hot)(
-        wants_of_higher, wants_of_lower, gathered
-    )
-    from_lower = lax.ppermute(to_higher, "group", higher)
-    from_higher = lax.ppermute(to_lower, "group", lower)
-    part, turned = call(
-        lateral_kernel,
-        [SMEM] * 3 + [VMEM] * 3,
+    for_near, turned = call(
+        sums_kernel,
+        [SMEM] * 3 + [VMEM] * 4,
         (
-            jax.ShapeDtypeStruct((NEAR * blocks + 8, values), jnp.float32),
+            jax.ShapeDtypeStruct((near, blocks, values), jnp.bfloat16),
             jax.ShapeDtypeStruct((blocks, width, points), basis.dtype),
         ),
-        10 * one_hot,
-    )(band_offsets, band_weight, radial_weight, wants, gathered, basis)
-    for_near = call(
-        near_kernel,
-        [VMEM] * 3,
-        jax.ShapeDtypeStruct((NEAR, blocks, values), jnp.bfloat16),
-        NEAR * blocks * values,
-    )(part, from_lower, from_higher)
+        14 * one_hot,
+    )(band_offsets, band_weight, radial_weight, wants, gathered, neighbour, basis)
     parts = lax.all_to_all(for_near, "cuts", 0, 0, axis_index_groups=sets, tiled=True)
     return call(
         expand_kernel,

time: 81.4 us -> 75.4 us (0.926)
  the two profiles are of different devices: /device:TPU:14 before, /device:TPU:24 now
where the time goes in v5:
time: 75.4 us; the launch traced here: 75.1 us
  blocking collectives  63.6 us (84%)
  starting transfers between devices  4.83 us (6%)
  Pallas kernels  3.19 us (4%)
  local copies, waits for them, and re-layouts  2.69 us (4%)
    all_gather x1, blocking collectives, body(): gathered = lax.all_gather(payload, 'cuts', axis_index_groups=shares)  41 us
    all_gather x1, blocking collectives, body(): wants = lax.all_gather(own, 'cuts', axis_index_groups=sets, tiled=True)  11.9 us
    all_to_all x1, blocking collectives, body(): lax.all_to_all(for_near, 'cuts', 0, 0, axis_index_groups=sets, tiled=True)  10.7 us
    ppermute x1, starting transfers between devices, body(): neighbour = lax.ppermute(gathered, ('group', 'cuts'), pairs)  4.83 us
    unnamed x14, local copies, waits for them, and re-layouts  2.69 us
    pallas_call x1, Pallas kernels, body(): call(sums_kernel, [SMEM] * 3 + [VMEM] * 4, (jax.ShapeDtypeStruct((near, b...  1.53 us
  transfers between devices with their start and end apart: 1, of which 0 were waited for; matrix products, arithmetic and copies ran while one was open for 0% of the time, Pallas kernels for 0%

profile of v5, /device:TPU:24, one launch (start us, length us, event | category | flops | bytes accessed | tf_op | source)
XLA Modules:
  0.0 75.1 jit_solution(2401462114969445183)
XLA Ops:
  0.0 0.0 copy-start.3
  0.0 0.7 bitcast_add_fusion.patch_ref
  0.7 0.0 copy-done.3
  0.7 0.0 copy-start
  0.7 1.2 %copy-done = bf16[1,32,128,128]{3,2,1,0:T(8,128)(2,1)S(1)} copy-done((bf16[1,32,128,128]{3,2,1,0:T(8,128)(2,1)S(1)}, bf16[1,32,128,128]{3,2,1,0:T(8,128)(2,1)}, u32[]{:S(2)}) %copy-start) | copy-done | bytes 1048600
  1.9 0.0 copy-start.2
  1.9 0.8 %copy-done.2 = f32[3,1,32,128]{3,2,1,0:T(8,128)S(1)} copy-done((f32[3,1,32,128]{3,2,1,0:T(8,128)S(1)}, f32[3,1,32,128]{3,2,1,0:T(8,128)}, u32[]{:S(2)}) %copy-start.2) | copy-done | bytes 49176
  2.7 0.0 copy-start.1
  2.7 0.6 shard_map.82
  3.4 41.0 %all-gather = bf16[1664,128]{1,0:T(8,128)(2,1)S(1)} all-gather(bf16[104,128]{1,0:T(8,128)(2,1)S(1)} %shard_map.82), channel_id=2, replica_groups={{0,1,8,9,16,17,24,25,32,33,40,41,48,49,56,57},{2,3,10,11,18,19,26,27,34..., dimensions={0}, use_global_device_ids=true | all-gather | bytes 452608 | tf_op jit(solution)/shard_map/all_gather | solution.py:190
  44.4 4.8 %collective-permute-start = (bf16[16,104,128]{2,1,0:T(8,128)(2,1)S(1)}, bf16[16,104,128]{2,1,0:T(8,128)(2,1)S(1)}, u32[]{:S(2)}, u32[]{:S(2)}) collective-permute-start(bf16[16,104,128]{2,1,0:T(8,128)(2,1)S(1)} %bitcast.5), channel_id=1, source_target_pairs={{1,65},{3,67},{5,69},{7,71},{9,73},{11,75},{13,77},{15,79},{17,81}... | collective-permute-start | bytes 1277960 | tf_op jit(solution)/shard_map/ppermute | solution.py:198
  49.2 0.0 copy-start.4
  49.2 11.9 %all-gather.1 = s32[8,1,32]{2,1,0:T(1,128)S(1)} all-gather(s32[1,1,32]{2,1,0:T(1,128)S(1)} %bitcast.8), channel_id=1, replica_groups={{0,1,2,3,4,5,6,7},{8,9,10,11,12,13,14,15},{16,17,18,19,20,21,22,23},{24..., dimensions={0}, use_global_device_ids=true | all-gather | bytes 1152 | tf_op jit(solution)/shard_map/all_gather | solution.py:173
  61.1 0.0 copy-start.5
  61.1 0.0 copy-start.6
  61.1 0.0 collective-permute-done.row_ref
  61.1 0.0 copy-done.1
  61.1 0.0 copy-done.4
  61.1 0.6 copy-done.5
  61.7 0.0 copy-done.6
  61.8 1.5 %shard_map.83 = (bf16[8,32,384]{2,1,0:T(8,128)(2,1)S(1)}, bf16[32,128,128]{2,1,0:T(8,128)(2,1)S(1)}) custom-call(s32[4]{0:T(128)S(1)} %copy-done.5, f32[3,4]{1,0:T(4,128)S(1)} %copy-done.4, f32[3]{0:T(128)S(1)} %copy-done.6, s32[8,32]{1,0:T(8,128)S(1)} %bitcast.7, bf16[16,104,128]{2,1,0:T(8,128)(2,1)S(1)} %bitcast.6, ...), custom_call_target="tpu_custom_call" | custom-call | flops 352321536 | bytes 2097152 | tf_op jit(solution)/shard_map/pallas_call | solution.py:200
  63.3 10.7 %all_to_all.5.parts_ref = bf16[8,32,384]{2,1,0:T(8,128)(2,1)S(1)} all-to-all(bf16[8,32,384]{2,1,0:T(8,128)(2,1)S(1)} %get-tuple-element.7), channel_id=1, replica_groups={{0,1,2,3,4,5,6,7},{8,9,10,11,12,13,14,15},{16,17,18,19,20,21,22,23},{24..., dimensions={0} | all-to-all | bytes 393216 | tf_op jit(solution)/shard_map/all_to_all | solution.py:209
  74.0 1.0 %shard_map.84 = f32[3,1,32,128]{3,2,1,0:T(8,128)} custom-call(bf16[8,32,384]{2,1,0:T(8,128)(2,1)S(1)} %all_to_all.5.parts_ref, bf16[32,128,128]{2,1,0:T(8,128)(2,1)S(1)} %get-tuple-element.8.turned_ref, s32[1,32]{1,0:T(1,128)S(1)} %copy-done.3), custom_call_target="tpu_custom_call" | custom-call | flops 3145728 | bytes 2097152 | tf_op jit(solution)/shard_map/pallas_call | solution.py:210
Async XLA Ops:
  0.0 0.7 copy-start.3
  0.7 1.2 %copy-start = (bf16[1,32,128,128]{3,2,1,0:T(8,128)(2,1)S(1)}, bf16[1,32,128,128]{3,2,1,0:T(8,128)(2,1)}, u32[]{:S(2)}) copy-start(bf16[1,32,128,128]{3,2,1,0:T(8,128)(2,1)} %basis_ref.1) | copy-start | bytes 3145732
  1.9 0.8 %copy-start.2 = (f32[3,1,32,128]{3,2,1,0:T(8,128)S(1)}, f32[3,1,32,128]{3,2,1,0:T(8,128)}, u32[]{:S(2)}) copy-start(f32[3,1,32,128]{3,2,1,0:T(8,128)} %gradient_hbm.1) | copy-start | bytes 147460
  2.7 58.4 %copy-start.1 = (bf16[1,32,128,128]{3,2,1,0:T(8,128)(2,1)S(1)}, bf16[1,32,128,128]{3,2,1,0:T(8,128)(2,1)}, u32[]{:S(2)}) copy-start(bf16[1,32,128,128]{3,2,1,0:T(8,128)(2,1)} %basis_ref.1) | copy-start | bytes 3145732
  44.4 16.7 %collective-permute-start = (bf16[16,104,128]{2,1,0:T(8,128)(2,1)S(1)}, bf16[16,104,128]{2,1,0:T(8,128)(2,1)S(1)}, u32[]{:S(2)}, u32[]{:S(2)}) collective-permute-start(bf16[16,104,128]{2,1,0:T(8,128)(2,1)S(1)} %bitcast.5), channel_id=1, source_target_pairs={{1,65},{3,67},{5,69},{7,71},{9,73},{11,75},{13,77},{15,79},{17,81}... | collective-permute-start | bytes 1277960 | tf_op jit(solution)/shard_map/ppermute | solution.py:198
  49.2 11.9 %copy-start.4 = (f32[3,4]{1,0:T(4,128)S(1)}, f32[3,4]{1,0:T(4,128)}, u32[]{:S(2)}) copy-start(f32[3,4]{1,0:T(4,128)} %band_ref.1) | copy-start | bytes 148
  61.1 0.7 copy-start.5
  61.1 0.7 copy-start.6

commit v6 on v5

--- a/solution.py
+++ b/solution.py
@@ -25,8 +25,12 @@
     return lax.broadcasted_iota(jnp.int32, (blocks, points), 1) < count
 
 
+def quarter(position):
+    return position // (NEAR * CORES) % 2 * CORES + position % CORES
+
+
 def project_kernel(
-    gradient_hbm, basis_hbm, patch_ref, valid_ref, payload_ref, gradient_ref, basis_ref, rows_ref, ids_ref, done
+    gradient_hbm, basis_hbm, patch_ref, valid_ref, early_ref, payload_ref, gradient_ref, basis_ref, rows_ref, ids_ref, done
 ):
     copies = [
         pltpu.make_async_copy(gradient_hbm, gradient_ref, done.at[0]),
@@ -39,9 +43,7 @@
     ids_ref[...] = jnp.zeros_like(ids_ref)
     ids_ref[0:1, 0:blocks] = patch_ref[0:1, :] // PD
     ids_ref[1:2, 0:blocks] = patch_ref[0:1, :] % PD
-    position = lax.axis_index("cuts")
-    quarter = (position // (NEAR * CORES)) % 2 * CORES + position % CORES
-    ids = pltpu.roll(ids_ref[...].astype(jnp.float32), quarter * blocks, 1)
+    ids = pltpu.roll(ids_ref[...].astype(jnp.float32), quarter(lax.axis_index("cuts")) * blocks, 1)
     payload_ref[params * blocks :, :] = ids.astype(jnp.bfloat16)
     copies[0].wait()
     for p in range(params):
@@ -87,31 +89,35 @@
     return [CORES * i + core for i in range(NEAR)]
 
 
-def sums_kernel(
-    offsets_ref, band_ref, radial_ref, wants_ref, all_ref, row_ref, basis_ref, out_ref, turned_ref
+def ids_of(ids, i):
+    place, slot = lax.axis_index("cuts"), 0
+    for bit in range(3):
+        mine = place // (1 << bit) % 2
+        other = i // (1 << bit) % 2
+        slot = slot + (mine + other - 2 * mine * other) * (1 << bit)
+    blocks = ids.shape[1]
+    return column(ids[pl.ds(slot, 1), :], blocks)
+
+
+def lateral_kernel(
+    offsets_ref, band_ref, radial_ref, early_ref, late_ref, all_ref, basis_ref, out_ref, turned_ref, ids_ref
 ):
     for b in range(turned_ref.shape[0]):
         turned_ref[b] = basis_ref[0, b].T
     width = all_ref.shape[2]
     params, bands = band_ref.shape
-    near, blocks, _ = out_ref.shape
+    _, blocks, _ = out_ref.shape
     count = NEAR * blocks
     patches = all_ref.shape[0] * NEAR * PD
-    wanted = jnp.concatenate([column(wants_ref[i : i + 1, :], blocks) for i in range(near)], axis=0)
-    beside = patch_sums(wanted, row_ref, params, blocks)
-    for p in range(params):
-        lanes = slice(p * width, (p + 1) * width)
-        radial = beside[:, lanes] * radial_ref[p]
-        for i in range(near):
-            out_ref[i, :, lanes] = radial[i * blocks : (i + 1) * blocks].astype(out_ref.dtype)
-    mine = jnp.concatenate([column(wants_ref[pl.ds(i, 1), :], blocks) for i in same_core()], axis=0)
+    ids_ref[...] = jnp.maximum(early_ref[...], late_ref[...])
+    mine = jnp.concatenate([ids_of(ids_ref, i) for i in same_core()], axis=0)
     wanted = [mine]
     for j in range(bands):
         moved = mine + offsets_ref[j]
         moved = jnp.where(moved < 0, moved + patches, moved)
         wanted.append(jnp.where(moved >= patches, moved - patches, moved))
     total = patch_sums(jnp.concatenate(wanted, axis=0), all_ref, params, blocks)
-    core = lax.axis_index("cuts") % CORES
+    out_ref[...] = jnp.zeros_like(out_ref)
     for p in range(params):
         lanes = slice(p * width, (p + 1) * width)
         part = total[:, lanes]
@@ -120,11 +126,22 @@
         for j in range(bands):
             shifted = part[(j + 1) * count : (j + 2) * count]
             smooth = smooth + band_ref[p, j] * (shifted - centre)
-        radial = beside[:, lanes] * radial_ref[p]
-        for i in range(NEAR):
-            both = [radial[(CORES * i + c) * blocks : (CORES * i + c + 1) * blocks] for c in range(CORES)]
-            added = jnp.where(core == 0, both[0], both[1]) + smooth[i * blocks : (i + 1) * blocks]
-            out_ref[pl.ds(CORES * i + core, 1), :, lanes] = added[None].astype(out_ref.dtype)
+        for n, i in enumerate(same_core()):
+            out_ref[pl.ds(i, 1), :, lanes] = smooth[None, n * blocks : (n + 1) * blocks]
+
+
+def radial_kernel(radial_ref, ids_ref, row_ref, part_ref, out_ref):
+    width = row_ref.shape[2]
+    near, blocks, values = out_ref.shape
+    params = values // width
+    wanted = jnp.concatenate([ids_of(ids_ref, i) for i in range(near)], axis=0)
+    total = patch_sums(wanted, row_ref, params, blocks)
+    for p in range(params):
+        lanes = slice(p * width, (p + 1) * width)
+        radial = total[:, lanes] * radial_ref[p]
+        for i in range(near):
+            part = part_ref[i, :, lanes] + radial[i * blocks : (i + 1) * blocks]
+            out_ref[i, :, lanes] = part.astype(out_ref.dtype)
 
 
 def expand_kernel(parts_ref, turned_ref, valid_ref, out_ref, rows_ref):
@@ -170,10 +187,18 @@
     near = NEAR * CORES
     sets = [list(range(first, first + near)) for first in range(0, cuts, near)]
     own = block_owner[:, :, 0] * PD + block_local
-    wants = lax.all_gather(own, "cuts", axis_index_groups=sets, tiled=True)
+
+    def wanted_near(own, chosen):
+        wants = own
+        for bit in range(3):
+            pairs = [(d, d ^ (1 << bit)) for d in range(cuts) if d // CORES in chosen]
+            wants = jnp.concatenate([wants, lax.ppermute(wants, "cuts", pairs)])
+        return wants
+
+    early = wanted_near(own, range(chips // 4))
     payload = call(
         project_kernel,
-        [HBM] * 2 + [VMEM] * 2,
+        [HBM] * 2 + [VMEM] * 3,
         jax.ShapeDtypeStruct((params * blocks + ID_ROWS, width), jnp.bfloat16),
         2 * blocks * params * points * width,
         [
@@ -183,7 +208,7 @@
             pltpu.VMEM((ID_ROWS, 128), jnp.int32),
             pltpu.SemaphoreType.DMA((2,)),
         ],
-    )(gradient, basis, own, valid_count)
+    )(gradient, basis, own, valid_count, early)
     shares = [
         [CORES * z + c for z in range(first, chips, NEAR) for c in range(CORES)] for first in range(NEAR)
     ]
@@ -196,16 +221,27 @@
         if 0 <= q < rows
     ]
     neighbour = lax.ppermute(gathered, ("group", "cuts"), pairs)
+    position = lax.axis_index("cuts")
+    place = (position // (NEAR * CORES) * CORES + position % CORES, params * blocks, quarter(position) * blocks)
+    ids = lax.dynamic_slice(gathered, place, (1, 2, blocks))[0].astype(jnp.int32)
+    late = wanted_near(ids[0:1] * PD + ids[1:2], range(chips // 4, chips))
     one_hot = blocks * blocks * cuts * values
-    for_near, turned = call(
-        sums_kernel,
+    part, turned, wants = call(
+        lateral_kernel,
         [SMEM] * 3 + [VMEM] * 4,
         (
-            jax.ShapeDtypeStruct((near, blocks, values), jnp.bfloat16),
+            jax.ShapeDtypeStruct((near, blocks, values), jnp.float32),
             jax.ShapeDtypeStruct((blocks, width, points), basis.dtype),
+            jax.ShapeDtypeStruct((near, blocks), jnp.int32),
         ),
-        14 * one_hot,
-    )(band_offsets, band_weight, radial_weight, wants, gathered, neighbour, basis)
+        10 * one_hot,
+    )(band_offsets, band_weight, radial_weight, early, late, gathered, basis)
+    for_near = call(
+        radial_kernel,
+        [SMEM] + [VMEM] * 3,
+        jax.ShapeDtypeStruct((near, blocks, values), jnp.bfloat16),
+        4 * one_hot,
+    )(radial_weight, wants, neighbour, part)
     parts = lax.all_to_all(for_near, "cuts", 0, 0, axis_index_groups=sets, tiled=True)
     return call(
         expand_kernel,

time: 75.4 us -> 76.4 us (1.013)
  the two profiles are of different devices: /device:TPU:24 before, /device:TPU:280 now
where the time goes in v6:
time: 76.4 us; the launch traced here: 76.1 us
  blocking collectives  46.9 us (61%)
  starting transfers between devices  18 us (24%)
  waiting for transfers between devices  4.22 us (6%)
  Pallas kernels  4.01 us (5%)
  local copies, waits for them, and re-layouts  1.87 us (2%)
  other arithmetic  0.82 us (1%)
    all_gather x1, blocking collectives, body(): gathered = lax.all_gather(payload, 'cuts', axis_index_groups=shares)  33.5 us
    all_to_all x1, blocking collectives, body(): lax.all_to_all(for_near, 'cuts', 0, 0, axis_index_groups=sets, tiled=True)  13.4 us
    ppermute x6, starting transfers between devices, wanted_near(): wants = jnp.concatenate([wants, lax.ppermute(wants, 'cuts', pairs)])  13.2 us
    ppermute x1, starting transfers between devices, body(): neighbour = lax.ppermute(gathered, ('group', 'cuts'), pairs)  4.83 us
    ppermute x6, waiting for transfers between devices, wanted_near(): wants = jnp.concatenate([wants, lax.ppermute(wants, 'cuts', pairs)])  4.22 us
    unnamed x14, local copies, waits for them, and re-layouts  1.87 us
  transfers between devices with their start and end apart: 7, of which 3 were waited for; matrix products, arithmetic and copies ran while one was open for 0% of the time, Pallas kernels for 2%

profile of v6, /device:TPU:280, one launch (start us, length us, event | category | flops | bytes accessed | tf_op | source)
XLA Modules:
  0.0 76.1 jit_solution(6641063844096158430)
XLA Ops:
  0.0 0.7 bitcast_add_fusion.patch_ref
  0.7 0.6 collective-permute-start
  1.3 0.0 copy-start.2
  1.4 0.0 collective-permute-done
  1.4 0.7 collective-permute-start.1
  2.1 0.0 collective-permute-done.1
  2.1 0.7 collective-permute-start.2
  2.8 0.0 copy-start.4
  2.8 0.0 collective-permute-done.2
  2.8 0.0 copy-done.2
  2.9 0.6 copy-done.4
  3.5 0.0 copy-start
  3.5 1.2 %copy-done = bf16[1,32,128,128]{3,2,1,0:T(8,128)(2,1)S(1)} copy-done((bf16[1,32,128,128]{3,2,1,0:T(8,128)(2,1)S(1)}, bf16[1,32,128,128]{3,2,1,0:T(8,128)(2,1)}, u32[]{:S(2)}) %copy-start) | copy-done | bytes 1048600
  4.7 0.0 copy-start.1
  4.7 0.6 shard_map.82
  5.3 33.5 %all-gather = bf16[1664,128]{1,0:T(8,128)(2,1)S(1)} all-gather(bf16[104,128]{1,0:T(8,128)(2,1)S(1)} %shard_map.82), channel_id=2, replica_groups={{0,1,8,9,16,17,24,25,32,33,40,41,48,49,56,57},{2,3,10,11,18,19,26,27,34..., dimensions={0}, use_global_device_ids=true | all-gather | bytes 452608 | tf_op jit(solution)/shard_map/all_gather | solution.py:215
  38.8 4.8 %collective-permute-start.6 = (bf16[16,104,128]{2,1,0:T(8,128)(2,1)S(1)}, bf16[16,104,128]{2,1,0:T(8,128)(2,1)S(1)}, u32[]{:S(2)}, u32[]{:S(2)}) collective-permute-start(bf16[16,104,128]{2,1,0:T(8,128)(2,1)S(1)} %bitcast.5), channel_id=1, source_target_pairs={{1,65},{3,67},{5,69},{7,71},{9,73},{11,75},{13,77},{15,79},{17,81}... | collective-permute-start | bytes 1277960 | tf_op jit(solution)/shard_map/ppermute | solution.py:223
  43.7 0.1 dynamic-slice_convert_fusion
  43.7 1.9 %collective-permute-start.3 = (s32[1,32]{1,0:T(1,128)S(1)}, s32[1,32]{1,0:T(1,128)S(1)}, u32[]{:S(2)}, u32[]{:S(2)}) collective-permute-start(s32[1,32]{1,0:T(1,128)S(1)} %add_bitcast_fusion), channel_id=1, source_target_pairs={{16,17},{17,16},{18,19},{19,18},{20,21},{21,20},{22,23},{23,22},{2... | collective-permute-start | bytes 392 | tf_op jit(solution)/shard_map/ppermute | solution.py:195
  45.7 1.1 %collective-permute-done.3 = s32[1,32]{1,0:T(1,128)S(1)} collective-permute-done((s32[1,32]{1,0:T(1,128)S(1)}, s32[1,32]{1,0:T(1,128)S(1)}, u32[]{:S(2)}, u32[]{:S(2)}) %collective-permute-start.3) | collective-permute-done | bytes 160 | tf_op jit(solution)/shard_map/ppermute | solution.py:195
  46.8 4.4 %collective-permute-start.4 = (s32[2,32]{1,0:T(2,128)S(1)}, s32[2,32]{1,0:T(2,128)S(1)}, u32[]{:S(2)}, u32[]{:S(2)}) collective-permute-start(s32[2,32]{1,0:T(2,128)S(1)} %pad_add_fusion.5), channel_id=1, source_target_pairs={{16,18},{17,19},{18,16},{19,17},{20,22},{21,23},{22,20},{23,21},{2... | collective-permute-start | bytes 776 | tf_op jit(solution)/shard_map/ppermute | solution.py:195
  51.1 1.5 %collective-permute-done.4 = s32[2,32]{1,0:T(2,128)S(1)} collective-permute-done((s32[2,32]{1,0:T(2,128)S(1)}, s32[2,32]{1,0:T(2,128)S(1)}, u32[]{:S(2)}, u32[]{:S(2)}) %collective-permute-start.4) | collective-permute-done | bytes 288 | tf_op jit(solution)/shard_map/ppermute | solution.py:195
  52.7 0.0 copy-start.3
  52.7 0.0 copy-start.5
  52.7 0.0 copy-start.6
  52.7 4.9 %collective-permute-start.5 = (s32[4,32]{1,0:T(4,128)S(1)}, s32[4,32]{1,0:T(4,128)S(1)}, u32[]{:S(2)}, u32[]{:S(2)}) collective-permute-start(s32[4,32]{1,0:T(4,128)S(1)} %pad_add_fusion.3), channel_id=1, source_target_pairs={{16,20},{17,21},{18,22},{19,23},{20,16},{21,17},{22,18},{23,19},{2... | collective-permute-start | bytes 1544 | tf_op jit(solution)/shard_map/ppermute | solution.py:195
  57.6 1.6 %collective-permute-done.5 = s32[4,32]{1,0:T(4,128)S(1)} collective-permute-done((s32[4,32]{1,0:T(4,128)S(1)}, s32[4,32]{1,0:T(4,128)S(1)}, u32[]{:S(2)}, u32[]{:S(2)}) %collective-permute-start.5) | collective-permute-done | bytes 544 | tf_op jit(solution)/shard_map/ppermute | solution.py:195
  59.2 0.0 copy-done.1
  59.3 0.0 copy-done.3
  59.3 0.0 copy-done.5
  59.3 0.0 copy-done.6
  59.3 1.3 %shard_map.83 = (f32[8,32,384]{2,1,0:T(8,128)S(1)}, bf16[32,128,128]{2,1,0:T(8,128)(2,1)S(1)}, s32[8,32]{1,0:T(8,128)S(1)}) custom-call(s32[4]{0:T(128)S(1)} %copy-done.6, f32[3,4]{1,0:T(4,128)S(1)} %copy-done.5, f32[3]{0:T(128)S(1)} %copy-done.3, s32[8,32]{1,0:T(8,128)S(1)} %pad_add_fusion.early_ref, s32[8,32]{1,0:T(8,128)S(1)} %pad_add_fusion.1.late_ref, ...), custom_call_target="tpu_custom_call" | custom-call | flops 251658240 | bytes 2097152 | tf_op jit(solution)/shard_map/pallas_call | solution.py:229
  60.6 0.0 collective-permute-done.6.row_ref
  60.6 1.1 %shard_map.84 = bf16[8,32,384]{2,1,0:T(8,128)(2,1)S(1)} custom-call(f32[3]{0:T(128)S(1)} %copy-done.3, s32[8,32]{1,0:T(8,128)S(1)} %get-tuple-element.8.ids_ref, bf16[16,104,128]{2,1,0:T(8,128)(2,1)S(1)} %collective-permute-done.6.row_ref, f32[8,32,384]{2,1,0:T(8,128)S(1)} %get-tuple-element.9.part_ref), custom_call_target="tpu_custom_call" | custom-call | flops 100663296 | bytes 2097152 | tf_op jit(solution)/shard_map/pallas_call | solution.py:239
  61.7 13.4 %all_to_all.5.parts_ref = bf16[8,32,384]{2,1,0:T(8,128)(2,1)S(1)} all-to-all(bf16[8,32,384]{2,1,0:T(8,128)(2,1)S(1)} %shard_map.84), channel_id=1, replica_groups={{0,1,2,3,4,5,6,7},{8,9,10,11,12,13,14,15},{16,17,18,19,20,21,22,23},{24..., dimensions={0} | all-to-all | bytes 393216 | tf_op jit(solution)/shard_map/all_to_all | solution.py:245
  75.0 1.0 %shard_map.85 = f32[3,1,32,128]{3,2,1,0:T(8,128)} custom-call(bf16[8,32,384]{2,1,0:T(8,128)(2,1)S(1)} %all_to_all.5.parts_ref, bf16[32,128,128]{2,1,0:T(8,128)(2,1)S(1)} %get-tuple-element.10.turned_ref, s32[1,32]{1,0:T(1,128)S(1)} %copy-done.4), custom_call_target="tpu_custom_call" | custom-call | flops 3145728 | bytes 2097152 | tf_op jit(solution)/shard_map/pallas_call | solution.py:246
  (7 shorter events, 0.1 us)
Async XLA Ops:
  0.7 0.7 collective-permute-start
  1.3 1.5 %copy-start.2 = (f32[3,1,32,128]{3,2,1,0:T(8,128)S(1)}, f32[3,1,32,128]{3,2,1,0:T(8,128)}, u32[]{:S(2)}) copy-start(f32[3,1,32,128]{3,2,1,0:T(8,128)} %gradient_hbm.1) | copy-start | bytes 147460
  1.4 0.7 collective-permute-start.1
  2.1 0.7 collective-permute-start.2
  2.8 0.7 copy-start.4
  3.5 1.2 %copy-start = (bf16[1,32,128,128]{3,2,1,0:T(8,128)(2,1)S(1)}, bf16[1,32,128,128]{3,2,1,0:T(8,128)(2,1)}, u32[]{:S(2)}) copy-start(bf16[1,32,128,128]{3,2,1,0:T(8,128)(2,1)} %basis_ref.1) | copy-start | bytes 3145732
  4.7 54.6 %copy-start.1 = (bf16[1,32,128,128]{3,2,1,0:T(8,128)(2,1)S(1)}, bf16[1,32,128,128]{3,2,1,0:T(8,128)(2,1)}, u32[]{:S(2)}) copy-start(bf16[1,32,128,128]{3,2,1,0:T(8,128)(2,1)} %basis_ref.1) | copy-start | bytes 3145732
  38.8 21.8 %collective-permute-start.6 = (bf16[16,104,128]{2,1,0:T(8,128)(2,1)S(1)}, bf16[16,104,128]{2,1,0:T(8,128)(2,1)S(1)}, u32[]{:S(2)}, u32[]{:S(2)}) collective-permute-start(bf16[16,104,128]{2,1,0:T(8,128)(2,1)S(1)} %bitcast.5), channel_id=1, source_target_pairs={{1,65},{3,67},{5,69},{7,71},{9,73},{11,75},{13,77},{15,79},{17,81}... | collective-permute-start | bytes 1277960 | tf_op jit(solution)/shard_map/ppermute | solution.py:223
  43.7 3.0 %collective-permute-start.3 = (s32[1,32]{1,0:T(1,128)S(1)}, s32[1,32]{1,0:T(1,128)S(1)}, u32[]{:S(2)}, u32[]{:S(2)}) collective-permute-start(s32[1,32]{1,0:T(1,128)S(1)} %add_bitcast_fusion), channel_id=1, source_target_pairs={{16,17},{17,16},{18,19},{19,18},{20,21},{21,20},{22,23},{23,22},{2... | collective-permute-start | bytes 392 | tf_op jit(solution)/shard_map/ppermute | solution.py:195
  46.8 5.9 %collective-permute-start.4 = (s32[2,32]{1,0:T(2,128)S(1)}, s32[2,32]{1,0:T(2,128)S(1)}, u32[]{:S(2)}, u32[]{:S(2)}) collective-permute-start(s32[2,32]{1,0:T(2,128)S(1)} %pad_add_fusion.5), channel_id=1, source_target_pairs={{16,18},{17,19},{18,16},{19,17},{20,22},{21,23},{22,20},{23,21},{2... | collective-permute-start | bytes 776 | tf_op jit(solution)/shard_map/ppermute | solution.py:195
  52.7 6.6 %copy-start.3 = (f32[3]{0:T(128)S(1)}, f32[3]{0:T(128)}, u32[]{:S(2)}) copy-start(f32[3]{0:T(128)} %radial_ref.3) | copy-start | bytes 40
  52.7 6.6 %copy-start.5 = (f32[3,4]{1,0:T(4,128)S(1)}, f32[3,4]{1,0:T(4,128)}, u32[]{:S(2)}) copy-start(f32[3,4]{1,0:T(4,128)} %band_ref.1) | copy-start | bytes 148
  52.7 6.6 %copy-start.6 = (s32[4]{0:T(128)S(1)}, s32[4]{0:T(128)}, u32[]{:S(2)}) copy-start(s32[4]{0:T(128)} %offsets_ref.1) | copy-start | bytes 52
  52.7 6.5 %collective-permute-start.5 = (s32[4,32]{1,0:T(4,128)S(1)}, s32[4,32]{1,0:T(4,128)S(1)}, u32[]{:S(2)}, u32[]{:S(2)}) collective-permute-start(s32[4,32]{1,0:T(4,128)S(1)} %pad_add_fusion.3), channel_id=1, source_target_pairs={{16,20},{17,21},{18,22},{19,23},{20,16},{21,17},{22,18},{23,19},{2... | collective-permute-start | bytes 1544 | tf_op jit(solution)/shard_map/ppermute | solution.py:195

commit v7 on v5

--- a/solution.py
+++ b/solution.py
@@ -170,7 +170,6 @@
     near = NEAR * CORES
     sets = [list(range(first, first + near)) for first in range(0, cuts, near)]
     own = block_owner[:, :, 0] * PD + block_local
-    wants = lax.all_gather(own, "cuts", axis_index_groups=sets, tiled=True)
     payload = call(
         project_kernel,
         [HBM] * 2 + [VMEM] * 2,
@@ -196,6 +195,17 @@
         if 0 <= q < rows
     ]
     neighbour = lax.ppermute(gathered, ("group", "cuts"), pairs)
+    position = lax.axis_index("cuts")
+    member, lane = position // (NEAR * CORES) * CORES, position // (NEAR * CORES) % 2 * CORES
+    ids = [
+        lax.dynamic_slice(
+            gathered, (member + c, params * blocks, (lane + c) * blocks), (1, 2, blocks)
+        )[0].astype(jnp.int32)
+        for c in range(CORES)
+    ]
+    ids = jnp.concatenate([each[0:1] * PD + each[1:2] for each in ids])
+    lines = [[at + CORES * i + c for i in range(NEAR)] for at in range(0, cuts, near) for c in range(CORES)]
+    wants = lax.all_gather(ids, "cuts", axis_index_groups=lines, tiled=True)
     one_hot = blocks * blocks * cuts * values
     for_near, turned = call(
         sums_kernel,

time: 75.4 us -> 74.7 us (level)
  blocking collectives: 63.6 us -> 62.8 us
    all_gather x1, blocking collectives: 11.9 us -> 11.1 us  [body(): wants = lax.all_gather(ids, 'cuts', axis_index_groups=lines, tiled=True)]
where the time goes in v7:
time: 74.7 us; the launch traced here: 74.4 us
  blocking collectives  62.8 us (84%)
  starting transfers between devices  4.83 us (6%)
  Pallas kernels  3.17 us (4%)
  local copies, waits for them, and re-layouts  2.69 us (4%)
  other arithmetic  0.79 us (1%)
    all_gather x1, blocking collectives, body(): gathered = lax.all_gather(payload, 'cuts', axis_index_groups=shares)  41 us
    all_gather x1, blocking collectives, body(): wants = lax.all_gather(ids, 'cuts', axis_index_groups=lines, tiled=True)  11.1 us
    all_to_all x1, blocking collectives, body(): lax.all_to_all(for_near, 'cuts', 0, 0, axis_index_groups=sets, tiled=True)  10.7 us
    ppermute x1, starting transfers between devices, body(): neighbour = lax.ppermute(gathered, ('group', 'cuts'), pairs)  4.83 us
    unnamed x14, local copies, waits for them, and re-layouts  2.69 us
    pallas_call x1, Pallas kernels, body(): call(sums_kernel, [SMEM] * 3 + [VMEM] * 4, (jax.ShapeDtypeStruct((near, b...  1.52 us
  transfers between devices with their start and end apart: 1, of which 0 were waited for; matrix products, arithmetic and copies ran while one was open for 0% of the time, Pallas kernels for 0%

profile of v7, /device:TPU:24, one launch (start us, length us, event | category | flops | bytes accessed | tf_op | source)
XLA Modules:
  0.0 74.4 jit_solution(10247942484345826602)
XLA Ops:
  0.0 0.0 copy-start.3
  0.0 0.7 bitcast_add_fusion.patch_ref
  0.7 0.0 copy-done.3
  0.7 0.0 copy-start
  0.7 1.2 %copy-done = bf16[1,32,128,128]{3,2,1,0:T(8,128)(2,1)S(1)} copy-done((bf16[1,32,128,128]{3,2,1,0:T(8,128)(2,1)S(1)}, bf16[1,32,128,128]{3,2,1,0:T(8,128)(2,1)}, u32[]{:S(2)}) %copy-start) | copy-done | bytes 1048600
  1.9 0.0 copy-start.2
  1.9 0.8 %copy-done.2 = f32[3,1,32,128]{3,2,1,0:T(8,128)S(1)} copy-done((f32[3,1,32,128]{3,2,1,0:T(8,128)S(1)}, f32[3,1,32,128]{3,2,1,0:T(8,128)}, u32[]{:S(2)}) %copy-start.2) | copy-done | bytes 49176
  2.7 0.0 copy-start.1
  2.7 0.6 shard_map.82
  3.4 41.0 %all-gather = bf16[1664,128]{1,0:T(8,128)(2,1)S(1)} all-gather(bf16[104,128]{1,0:T(8,128)(2,1)S(1)} %shard_map.82), channel_id=2, replica_groups={{0,1,8,9,16,17,24,25,32,33,40,41,48,49,56,57},{2,3,10,11,18,19,26,27,34..., dimensions={0}, use_global_device_ids=true | all-gather | bytes 452608 | tf_op jit(solution)/shard_map/all_gather | solution.py:189
  44.4 4.8 %collective-permute-start = (bf16[16,104,128]{2,1,0:T(8,128)(2,1)S(1)}, bf16[16,104,128]{2,1,0:T(8,128)(2,1)S(1)}, u32[]{:S(2)}, u32[]{:S(2)}) collective-permute-start(bf16[16,104,128]{2,1,0:T(8,128)(2,1)S(1)} %bitcast.10), channel_id=1, source_target_pairs={{1,65},{3,67},{5,69},{7,71},{9,73},{11,75},{13,77},{15,79},{17,81}... | collective-permute-start | bytes 1277960 | tf_op jit(solution)/shard_map/ppermute | solution.py:197
  49.2 0.1 fusion
  49.4 0.0 copy-start.4
  49.4 11.1 %all-gather.1 = s32[4,2,32]{2,1,0:T(2,128)S(1)} all-gather(s32[1,2,32]{2,1,0:T(2,128)S(1)} %add_bitcast_fusion), channel_id=1, replica_groups={{0,2,4,6},{1,3,5,7},{8,10,12,14},{9,11,13,15},{16,18,20,22},{17,19,21,2..., dimensions={0}, use_global_device_ids=true | all-gather | bytes 1280 | tf_op jit(solution)/shard_map/all_gather | solution.py:208
  60.5 0.0 copy-start.5
  60.5 0.0 copy-start.6
  60.5 0.0 collective-permute-done.row_ref
  60.5 0.0 copy-done.1
  60.5 0.0 copy-done.4
  60.5 0.6 copy-done.5
  61.1 0.0 copy-done.6
  61.1 1.5 %shard_map.83 = (bf16[8,32,384]{2,1,0:T(8,128)(2,1)S(1)}, bf16[32,128,128]{2,1,0:T(8,128)(2,1)S(1)}) custom-call(s32[4]{0:T(128)S(1)} %copy-done.5, f32[3,4]{1,0:T(4,128)S(1)} %copy-done.4, f32[3]{0:T(128)S(1)} %copy-done.6, s32[8,32]{1,0:T(8,128)S(1)} %bitcast.13, bf16[16,104,128]{2,1,0:T(8,128)(2,1)S(1)} %bitcast.12, ...), custom_call_target="tpu_custom_call" | custom-call | flops 352321536 | bytes 2097152 | tf_op jit(solution)/shard_map/pallas_call | solution.py:210
  62.7 10.7 %all_to_all.5.parts_ref = bf16[8,32,384]{2,1,0:T(8,128)(2,1)S(1)} all-to-all(bf16[8,32,384]{2,1,0:T(8,128)(2,1)S(1)} %get-tuple-element.7), channel_id=1, replica_groups={{0,1,2,3,4,5,6,7},{8,9,10,11,12,13,14,15},{16,17,18,19,20,21,22,23},{24..., dimensions={0} | all-to-all | bytes 393216 | tf_op jit(solution)/shard_map/all_to_all | solution.py:219
  73.4 1.0 %shard_map.84 = f32[3,1,32,128]{3,2,1,0:T(8,128)} custom-call(bf16[8,32,384]{2,1,0:T(8,128)(2,1)S(1)} %all_to_all.5.parts_ref, bf16[32,128,128]{2,1,0:T(8,128)(2,1)S(1)} %get-tuple-element.8.turned_ref, s32[1,32]{1,0:T(1,128)S(1)} %copy-done.3), custom_call_target="tpu_custom_call" | custom-call | flops 3145728 | bytes 2097152 | tf_op jit(solution)/shard_map/pallas_call | solution.py:220
  (2 shorter events, 0.0 us)
Async XLA Ops:
  0.0 0.7 copy-start.3
  0.7 1.2 %copy-start = (bf16[1,32,128,128]{3,2,1,0:T(8,128)(2,1)S(1)}, bf16[1,32,128,128]{3,2,1,0:T(8,128)(2,1)}, u32[]{:S(2)}) copy-start(bf16[1,32,128,128]{3,2,1,0:T(8,128)(2,1)} %basis_ref.1) | copy-start | bytes 3145732
  1.9 0.8 %copy-start.2 = (f32[3,1,32,128]{3,2,1,0:T(8,128)S(1)}, f32[3,1,32,128]{3,2,1,0:T(8,128)}, u32[]{:S(2)}) copy-start(f32[3,1,32,128]{3,2,1,0:T(8,128)} %gradient_hbm.1) | copy-start | bytes 147460
  2.7 57.8 %copy-start.1 = (bf16[1,32,128,128]{3,2,1,0:T(8,128)(2,1)S(1)}, bf16[1,32,128,128]{3,2,1,0:T(8,128)(2,1)}, u32[]{:S(2)}) copy-start(bf16[1,32,128,128]{3,2,1,0:T(8,128)(2,1)} %basis_ref.1) | copy-start | bytes 3145732
  44.4 16.1 %collective-permute-start = (bf16[16,104,128]{2,1,0:T(8,128)(2,1)S(1)}, bf16[16,104,128]{2,1,0:T(8,128)(2,1)S(1)}, u32[]{:S(2)}, u32[]{:S(2)}) collective-permute-start(bf16[16,104,128]{2,1,0:T(8,128)(2,1)S(1)} %bitcast.10), channel_id=1, source_target_pairs={{1,65},{3,67},{5,69},{7,71},{9,73},{11,75},{13,77},{15,79},{17,81}... | collective-permute-start | bytes 1277960 | tf_op jit(solution)/shard_map/ppermute | solution.py:197
  49.4 11.1 %copy-start.4 = (f32[3,4]{1,0:T(4,128)S(1)}, f32[3,4]{1,0:T(4,128)}, u32[]{:S(2)}) copy-start(f32[3,4]{1,0:T(4,128)} %band_ref.1) | copy-start | bytes 148
  60.5 0.7 copy-start.5
  60.5 0.7 copy-start.6

commit v8 on v7

--- a/solution.py
+++ b/solution.py
@@ -8,7 +8,7 @@
 PD = 16
 CORES = 2
 NEAR = 4
-ID_ROWS = 8
+ID_ROWS = 16
 
 
 def column(row, count):

time: 74.7 us -> 75 us (level)
  no operation moved by 1% of the time
where the time goes in v8:
time: 75 us; the launch traced here: 74.7 us
  blocking collectives  63.1 us (84%)
  starting transfers between devices  4.83 us (6%)
  Pallas kernels  3.19 us (4%)
  local copies, waits for them, and re-layouts  2.69 us (4%)
  other arithmetic  0.79 us (1%)
    all_gather x1, blocking collectives, body(): gathered = lax.all_gather(payload, 'cuts', axis_index_groups=shares)  41.2 us
    all_gather x1, blocking collectives, body(): wants = lax.all_gather(ids, 'cuts', axis_index_groups=lines, tiled=True)  11.2 us
    all_to_all x1, blocking collectives, body(): lax.all_to_all(for_near, 'cuts', 0, 0, axis_index_groups=sets, tiled=True)  10.7 us
    ppermute x1, starting transfers between devices, body(): neighbour = lax.ppermute(gathered, ('group', 'cuts'), pairs)  4.83 us
    unnamed x14, local copies, waits for them, and re-layouts  2.69 us
    pallas_call x1, Pallas kernels, body(): call(sums_kernel, [SMEM] * 3 + [VMEM] * 4, (jax.ShapeDtypeStruct((near, b...  1.53 us
  transfers between devices with their start and end apart: 1, of which 0 were waited for; matrix products, arithmetic and copies ran while one was open for 0% of the time, Pallas kernels for 0%

profile of v8, /device:TPU:24, one launch (start us, length us, event | category | flops | bytes accessed | tf_op | source)
XLA Modules:
  0.0 74.7 jit_solution(1208940923797693930)
XLA Ops:
  0.0 0.0 copy-start.3
  0.0 0.7 bitcast_add_fusion.patch_ref
  0.7 0.0 copy-done.3
  0.7 0.0 copy-start
  0.7 1.2 %copy-done = bf16[1,32,128,128]{3,2,1,0:T(8,128)(2,1)S(1)} copy-done((bf16[1,32,128,128]{3,2,1,0:T(8,128)(2,1)S(1)}, bf16[1,32,128,128]{3,2,1,0:T(8,128)(2,1)}, u32[]{:S(2)}) %copy-start) | copy-done | bytes 1048600
  1.9 0.0 copy-start.2
  1.9 0.8 %copy-done.2 = f32[3,1,32,128]{3,2,1,0:T(8,128)S(1)} copy-done((f32[3,1,32,128]{3,2,1,0:T(8,128)S(1)}, f32[3,1,32,128]{3,2,1,0:T(8,128)}, u32[]{:S(2)}) %copy-start.2) | copy-done | bytes 49176
  2.7 0.0 copy-start.1
  2.7 0.6 shard_map.82
  3.4 41.2 %all-gather = bf16[1792,128]{1,0:T(8,128)(2,1)S(1)} all-gather(bf16[112,128]{1,0:T(8,128)(2,1)S(1)} %shard_map.82), channel_id=2, replica_groups={{0,1,8,9,16,17,24,25,32,33,40,41,48,49,56,57},{2,3,10,11,18,19,26,27,34..., dimensions={0}, use_global_device_ids=true | all-gather | bytes 487424 | tf_op jit(solution)/shard_map/all_gather | solution.py:189
  44.6 4.8 %collective-permute-start = (bf16[16,112,128]{2,1,0:T(8,128)(2,1)S(1)}, bf16[16,112,128]{2,1,0:T(8,128)(2,1)S(1)}, u32[]{:S(2)}, u32[]{:S(2)}) collective-permute-start(bf16[16,112,128]{2,1,0:T(8,128)(2,1)S(1)} %bitcast.10), channel_id=1, source_target_pairs={{1,65},{3,67},{5,69},{7,71},{9,73},{11,75},{13,77},{15,79},{17,81}... | collective-permute-start | bytes 1376264 | tf_op jit(solution)/shard_map/ppermute | solution.py:197
  49.5 0.1 fusion
  49.6 0.0 copy-start.4
  49.6 11.2 %all-gather.1 = s32[4,2,32]{2,1,0:T(2,128)S(1)} all-gather(s32[1,2,32]{2,1,0:T(2,128)S(1)} %add_bitcast_fusion), channel_id=1, replica_groups={{0,2,4,6},{1,3,5,7},{8,10,12,14},{9,11,13,15},{16,18,20,22},{17,19,21,2..., dimensions={0}, use_global_device_ids=true | all-gather | bytes 1280 | tf_op jit(solution)/shard_map/all_gather | solution.py:208
  60.7 0.0 copy-start.5
  60.7 0.0 copy-start.6
  60.7 0.0 collective-permute-done.row_ref
  60.7 0.0 copy-done.1
  60.8 0.0 copy-done.4
  60.8 0.6 copy-done.5
  61.4 0.0 copy-done.6
  61.4 1.5 %shard_map.83 = (bf16[8,32,384]{2,1,0:T(8,128)(2,1)S(1)}, bf16[32,128,128]{2,1,0:T(8,128)(2,1)S(1)}) custom-call(s32[4]{0:T(128)S(1)} %copy-done.5, f32[3,4]{1,0:T(4,128)S(1)} %copy-done.4, f32[3]{0:T(128)S(1)} %copy-done.6, s32[8,32]{1,0:T(8,128)S(1)} %bitcast.13, bf16[16,112,128]{2,1,0:T(8,128)(2,1)S(1)} %bitcast.12, ...), custom_call_target="tpu_custom_call" | custom-call | flops 352321536 | bytes 2097152 | tf_op jit(solution)/shard_map/pallas_call | solution.py:210
  62.9 10.7 %all_to_all.5.parts_ref = bf16[8,32,384]{2,1,0:T(8,128)(2,1)S(1)} all-to-all(bf16[8,32,384]{2,1,0:T(8,128)(2,1)S(1)} %get-tuple-element.7), channel_id=1, replica_groups={{0,1,2,3,4,5,6,7},{8,9,10,11,12,13,14,15},{16,17,18,19,20,21,22,23},{24..., dimensions={0} | all-to-all | bytes 393216 | tf_op jit(solution)/shard_map/all_to_all | solution.py:219
  73.7 1.0 %shard_map.84 = f32[3,1,32,128]{3,2,1,0:T(8,128)} custom-call(bf16[8,32,384]{2,1,0:T(8,128)(2,1)S(1)} %all_to_all.5.parts_ref, bf16[32,128,128]{2,1,0:T(8,128)(2,1)S(1)} %get-tuple-element.8.turned_ref, s32[1,32]{1,0:T(1,128)S(1)} %copy-done.3), custom_call_target="tpu_custom_call" | custom-call | flops 3145728 | bytes 2097152 | tf_op jit(solution)/shard_map/pallas_call | solution.py:220
  (2 shorter events, 0.0 us)
Async XLA Ops:
  0.0 0.7 copy-start.3
  0.7 1.2 %copy-start = (bf16[1,32,128,128]{3,2,1,0:T(8,128)(2,1)S(1)}, bf16[1,32,128,128]{3,2,1,0:T(8,128)(2,1)}, u32[]{:S(2)}) copy-start(bf16[1,32,128,128]{3,2,1,0:T(8,128)(2,1)} %basis_ref.1) | copy-start | bytes 3145732
  1.9 0.8 %copy-start.2 = (f32[3,1,32,128]{3,2,1,0:T(8,128)S(1)}, f32[3,1,32,128]{3,2,1,0:T(8,128)}, u32[]{:S(2)}) copy-start(f32[3,1,32,128]{3,2,1,0:T(8,128)} %gradient_hbm.1) | copy-start | bytes 147460
  2.7 58.0 %copy-start.1 = (bf16[1,32,128,128]{3,2,1,0:T(8,128)(2,1)S(1)}, bf16[1,32,128,128]{3,2,1,0:T(8,128)(2,1)}, u32[]{:S(2)}) copy-start(bf16[1,32,128,128]{3,2,1,0:T(8,128)(2,1)} %basis_ref.1) | copy-start | bytes 3145732
  44.6 16.2 %collective-permute-start = (bf16[16,112,128]{2,1,0:T(8,128)(2,1)S(1)}, bf16[16,112,128]{2,1,0:T(8,128)(2,1)S(1)}, u32[]{:S(2)}, u32[]{:S(2)}) collective-permute-start(bf16[16,112,128]{2,1,0:T(8,128)(2,1)S(1)} %bitcast.10), channel_id=1, source_target_pairs={{1,65},{3,67},{5,69},{7,71},{9,73},{11,75},{13,77},{15,79},{17,81}... | collective-permute-start | bytes 1376264 | tf_op jit(solution)/shard_map/ppermute | solution.py:197
  49.6 11.2 %copy-start.4 = (f32[3,4]{1,0:T(4,128)S(1)}, f32[3,4]{1,0:T(4,128)}, u32[]{:S(2)}) copy-start(f32[3,4]{1,0:T(4,128)} %band_ref.1) | copy-start | bytes 148
  60.7 0.7 copy-start.5
  60.7 0.7 copy-start.6

commit v9 on v8

--- a/solution.py
+++ b/solution.py
@@ -26,7 +26,7 @@
 
 
 def project_kernel(
-    gradient_hbm, basis_hbm, patch_ref, valid_ref, payload_ref, gradient_ref, basis_ref, rows_ref, ids_ref, done
+    gradient_hbm, basis_hbm, patch_ref, valid_ref, offsets_ref, payload_ref, shifts_ref, gradient_ref, basis_ref, rows_ref, ids_ref, done
 ):
     copies = [
         pltpu.make_async_copy(gradient_hbm, gradient_ref, done.at[0]),
@@ -36,6 +36,8 @@
         copy.start()
     params, _, blocks, points = gradient_ref.shape
     inside = inside_mask(valid_ref, blocks, points)
+    for j in range(offsets_ref.shape[0]):
+        shifts_ref[j : j + 1, :] = jnp.full((1, 128), offsets_ref[j], jnp.int32)
     ids_ref[...] = jnp.zeros_like(ids_ref)
     ids_ref[0:1, 0:blocks] = patch_ref[0:1, :] // PD
     ids_ref[1:2, 0:blocks] = patch_ref[0:1, :] % PD
@@ -88,7 +90,7 @@
 
 
 def sums_kernel(
-    offsets_ref, band_ref, radial_ref, wants_ref, all_ref, row_ref, basis_ref, out_ref, turned_ref
+    shifts_ref, band_ref, radial_ref, wants_ref, all_ref, row_ref, basis_ref, out_ref, turned_ref
 ):
     for b in range(turned_ref.shape[0]):
         turned_ref[b] = basis_ref[0, b].T
@@ -107,7 +109,7 @@
     mine = jnp.concatenate([column(wants_ref[pl.ds(i, 1), :], blocks) for i in same_core()], axis=0)
     wanted = [mine]
     for j in range(bands):
-        moved = mine + offsets_ref[j]
+        moved = mine + shifts_ref[j : j + 1, 0:1]
         moved = jnp.where(moved < 0, moved + patches, moved)
         wanted.append(jnp.where(moved >= patches, moved - patches, moved))
     total = patch_sums(jnp.concatenate(wanted, axis=0), all_ref, params, blocks)
@@ -170,10 +172,13 @@
     near = NEAR * CORES
     sets = [list(range(first, first + near)) for first in range(0, cuts, near)]
     own = block_owner[:, :, 0] * PD + block_local
-    payload = call(
+    payload, shifts = call(
         project_kernel,
-        [HBM] * 2 + [VMEM] * 2,
-        jax.ShapeDtypeStruct((params * blocks + ID_ROWS, width), jnp.bfloat16),
+        [HBM] * 2 + [VMEM] * 2 + [SMEM],
+        (
+            jax.ShapeDtypeStruct((params * blocks + ID_ROWS, width), jnp.bfloat16),
+            jax.ShapeDtypeStruct((band_offsets.shape[0], 128), jnp.int32),
+        ),
         2 * blocks * params * points * width,
         [
             pltpu.VMEM(gradient.shape, gradient.dtype),
@@ -182,7 +187,7 @@
             pltpu.VMEM((ID_ROWS, 128), jnp.int32),
             pltpu.SemaphoreType.DMA((2,)),
         ],
-    )(gradient, basis, own, valid_count)
+    )(gradient, basis, own, valid_count, band_offsets)
     shares = [
         [CORES * z + c for z in range(first, chips, NEAR) for c in range(CORES)] for first in range(NEAR)
     ]
@@ -209,13 +214,13 @@
     one_hot = blocks * blocks * cuts * values
     for_near, turned = call(
         sums_kernel,
-        [SMEM] * 3 + [VMEM] * 4,
+        [VMEM] + [SMEM] * 2 + [VMEM] * 4,
         (
             jax.ShapeDtypeStruct((near, blocks, values), jnp.bfloat16),
             jax.ShapeDtypeStruct((blocks, width, points), basis.dtype),
         ),
         14 * one_hot,
-    )(band_offsets, band_weight, radial_weight, wants, gathered, neighbour, basis)
+    )(shifts, band_weight, radial_weight, wants, gathered, neighbour, basis)
     parts = lax.all_to_all(for_near, "cuts", 0, 0, axis_index_groups=sets, tiled=True)
     return call(
         expand_kernel,

time: 75 us -> 75.6 us (level)
  no operation moved by 1% of the time
where the time goes in v9:
time: 75.6 us; the launch traced here: 75.3 us
  blocking collectives  63.1 us (83%)
  starting transfers between devices  4.83 us (6%)
  Pallas kernels  3.75 us (5%)
  local copies, waits for them, and re-layouts  2.7 us (4%)
  other arithmetic  0.81 us (1%)
    all_gather x1, blocking collectives, body(): gathered = lax.all_gather(payload, 'cuts', axis_index_groups=shares)  41.2 us
    all_gather x1, blocking collectives, body(): wants = lax.all_gather(ids, 'cuts', axis_index_groups=lines, tiled=True)  11.2 us
    all_to_all x1, blocking collectives, body(): lax.all_to_all(for_near, 'cuts', 0, 0, axis_index_groups=sets, tiled=True)  10.7 us
    ppermute x1, starting transfers between devices, body(): neighbour = lax.ppermute(gathered, ('group', 'cuts'), pairs)  4.83 us
    unnamed x14, local copies, waits for them, and re-layouts  2.7 us
    pallas_call x1, Pallas kernels, body(): call(sums_kernel, [VMEM] + [SMEM] * 2 + [VMEM] * 4, (jax.ShapeDtypeStruct...  1.52 us
  transfers between devices with their start and end apart: 1, of which 0 were waited for; matrix products, arithmetic and copies ran while one was open for 0% of the time, Pallas kernels for 0%

profile of v9, /device:TPU:24, one launch (start us, length us, event | category | flops | bytes accessed | tf_op | source)
XLA Modules:
  0.0 75.3 jit_solution(9641485902171605968)
XLA Ops:
  0.0 0.0 copy-start.3
  0.0 0.0 copy-start.5
  0.0 0.7 bitcast_add_fusion.patch_ref
  0.7 0.0 copy-done.3
  0.7 0.0 copy-done.5
  0.7 0.0 copy-start
  0.7 1.2 %copy-done = bf16[1,32,128,128]{3,2,1,0:T(8,128)(2,1)S(1)} copy-done((bf16[1,32,128,128]{3,2,1,0:T(8,128)(2,1)S(1)}, bf16[1,32,128,128]{3,2,1,0:T(8,128)(2,1)}, u32[]{:S(2)}) %copy-start) | copy-done | bytes 1048600
  1.9 0.0 copy-start.2
  1.9 0.8 %copy-done.2 = f32[3,1,32,128]{3,2,1,0:T(8,128)S(1)} copy-done((f32[3,1,32,128]{3,2,1,0:T(8,128)S(1)}, f32[3,1,32,128]{3,2,1,0:T(8,128)}, u32[]{:S(2)}) %copy-start.2) | copy-done | bytes 49176
  2.7 0.0 copy-start.1
  2.7 1.2 %shard_map.82 = (bf16[112,128]{1,0:T(8,128)(2,1)S(1)}, s32[4,128]{1,0:T(4,128)S(1)}) custom-call(f32[3,1,32,128]{3,2,1,0:T(8,128)S(1)} %copy-done.2, bf16[1,32,128,128]{3,2,1,0:T(8,128)(2,1)S(1)} %copy-done, s32[1,32]{1,0:T(1,128)S(1)} %bitcast_add_fusion.patch_ref, s32[1,32]{1,0:T(1,128)S(1)} %copy-done.3, s32[4]{0:T(128)S(1)} %copy-done.5), custom_call_target="tpu_custom_call" | custom-call | flops 3145728 | bytes 2097152 | tf_op jit(solution)/shard_map/pallas_call | solution.py:175
  3.9 41.2 %all-gather = bf16[1792,128]{1,0:T(8,128)(2,1)S(1)} all-gather(bf16[112,128]{1,0:T(8,128)(2,1)S(1)} %get-tuple-element.10), channel_id=2, replica_groups={{0,1,8,9,16,17,24,25,32,33,40,41,48,49,56,57},{2,3,10,11,18,19,26,27,34..., dimensions={0}, use_global_device_ids=true | all-gather | bytes 487424 | tf_op jit(solution)/shard_map/all_gather | solution.py:194
  45.1 4.8 %collective-permute-start = (bf16[16,112,128]{2,1,0:T(8,128)(2,1)S(1)}, bf16[16,112,128]{2,1,0:T(8,128)(2,1)S(1)}, u32[]{:S(2)}, u32[]{:S(2)}) collective-permute-start(bf16[16,112,128]{2,1,0:T(8,128)(2,1)S(1)} %bitcast.10), channel_id=1, source_target_pairs={{1,65},{3,67},{5,69},{7,71},{9,73},{11,75},{13,77},{15,79},{17,81}... | collective-permute-start | bytes 1376264 | tf_op jit(solution)/shard_map/ppermute | solution.py:202
  50.0 0.1 fusion
  50.1 11.2 %all-gather.1 = s32[4,2,32]{2,1,0:T(2,128)S(1)} all-gather(s32[1,2,32]{2,1,0:T(2,128)S(1)} %add_bitcast_fusion), channel_id=1, replica_groups={{0,2,4,6},{1,3,5,7},{8,10,12,14},{9,11,13,15},{16,18,20,22},{17,19,21,2..., dimensions={0}, use_global_device_ids=true | all-gather | bytes 1280 | tf_op jit(solution)/shard_map/all_gather | solution.py:213
  61.3 0.0 copy-start.4
  61.3 0.0 collective-permute-done.row_ref
  61.3 0.0 copy-start.6
  61.3 0.0 copy-done.1
  61.3 0.7 copy-done.4
  62.0 0.0 copy-done.6
  62.0 1.5 %shard_map.83 = (bf16[8,32,384]{2,1,0:T(8,128)(2,1)S(1)}, bf16[32,128,128]{2,1,0:T(8,128)(2,1)S(1)}) custom-call(s32[4,128]{1,0:T(4,128)S(1)} %get-tuple-element.9.shifts_ref, f32[3,4]{1,0:T(4,128)S(1)} %copy-done.4, f32[3]{0:T(128)S(1)} %copy-done.6, s32[8,32]{1,0:T(8,128)S(1)} %bitcast.13, bf16[16,112,128]{2,1,0:T(8,128)(2,1)S(1)} %bitcast.12, ...), custom_call_target="tpu_custom_call" | custom-call | flops 352321536 | bytes 2097152 | tf_op jit(solution)/shard_map/pallas_call | solution.py:215
  63.5 10.7 %all_to_all.5.parts_ref = bf16[8,32,384]{2,1,0:T(8,128)(2,1)S(1)} all-to-all(bf16[8,32,384]{2,1,0:T(8,128)(2,1)S(1)} %get-tuple-element.11), channel_id=1, replica_groups={{0,1,2,3,4,5,6,7},{8,9,10,11,12,13,14,15},{16,17,18,19,20,21,22,23},{24..., dimensions={0} | all-to-all | bytes 393216 | tf_op jit(solution)/shard_map/all_to_all | solution.py:224
  74.3 1.0 %shard_map.84 = f32[3,1,32,128]{3,2,1,0:T(8,128)} custom-call(bf16[8,32,384]{2,1,0:T(8,128)(2,1)S(1)} %all_to_all.5.parts_ref, bf16[32,128,128]{2,1,0:T(8,128)(2,1)S(1)} %get-tuple-element.12.turned_ref, s32[1,32]{1,0:T(1,128)S(1)} %copy-done.3), custom_call_target="tpu_custom_call" | custom-call | flops 3145728 | bytes 2097152 | tf_op jit(solution)/shard_map/pallas_call | solution.py:225
  (2 shorter events, 0.0 us)
Async XLA Ops:
  0.0 0.7 copy-start.3
  0.0 0.7 copy-start.5
  0.7 1.2 %copy-start = (bf16[1,32,128,128]{3,2,1,0:T(8,128)(2,1)S(1)}, bf16[1,32,128,128]{3,2,1,0:T(8,128)(2,1)}, u32[]{:S(2)}) copy-start(bf16[1,32,128,128]{3,2,1,0:T(8,128)(2,1)} %basis_ref.1) | copy-start | bytes 3145732
  1.9 0.8 %copy-start.2 = (f32[3,1,32,128]{3,2,1,0:T(8,128)S(1)}, f32[3,1,32,128]{3,2,1,0:T(8,128)}, u32[]{:S(2)}) copy-start(f32[3,1,32,128]{3,2,1,0:T(8,128)} %gradient_hbm.1) | copy-start | bytes 147460
  2.7 58.6 %copy-start.1 = (bf16[1,32,128,128]{3,2,1,0:T(8,128)(2,1)S(1)}, bf16[1,32,128,128]{3,2,1,0:T(8,128)(2,1)}, u32[]{:S(2)}) copy-start(bf16[1,32,128,128]{3,2,1,0:T(8,128)(2,1)} %basis_ref.1) | copy-start | bytes 3145732
  45.1 16.2 %collective-permute-start = (bf16[16,112,128]{2,1,0:T(8,128)(2,1)S(1)}, bf16[16,112,128]{2,1,0:T(8,128)(2,1)S(1)}, u32[]{:S(2)}, u32[]{:S(2)}) collective-permute-start(bf16[16,112,128]{2,1,0:T(8,128)(2,1)S(1)} %bitcast.10), channel_id=1, source_target_pairs={{1,65},{3,67},{5,69},{7,71},{9,73},{11,75},{13,77},{15,79},{17,81}... | collective-permute-start | bytes 1376264 | tf_op jit(solution)/shard_map/ppermute | solution.py:202
  61.3 0.7 copy-start.4
  61.3 0.7 copy-start.6

commit v10 on v8

--- a/solution.py
+++ b/solution.py
@@ -57,7 +57,7 @@
 def patch_sums(wanted, all_ref, params, blocks):
     members, _, width = all_ref.shape
     group = 128 // blocks
-    tile = 2 * group
+    tile = 4 * group
     total = jnp.zeros((wanted.shape[0], params * width), jnp.float32)
     for start in range(0, members, tile):
         ids = []

time: 75 us -> 75 us (level)
  no operation moved by 1% of the time
where the time goes in v10:
time: 75 us; the launch traced here: 74.7 us
  blocking collectives  63.1 us (84%)
  starting transfers between devices  4.83 us (6%)
  Pallas kernels  3.18 us (4%)
  local copies, waits for them, and re-layouts  2.69 us (4%)
  other arithmetic  0.79 us (1%)
    all_gather x1, blocking collectives, body(): gathered = lax.all_gather(payload, 'cuts', axis_index_groups=shares)  41.2 us
    all_gather x1, blocking collectives, body(): wants = lax.all_gather(ids, 'cuts', axis_index_groups=lines, tiled=True)  11.2 us
    all_to_all x1, blocking collectives, body(): lax.all_to_all(for_near, 'cuts', 0, 0, axis_index_groups=sets, tiled=True)  10.7 us
    ppermute x1, starting transfers between devices, body(): neighbour = lax.ppermute(gathered, ('group', 'cuts'), pairs)  4.83 us
    unnamed x14, local copies, waits for them, and re-layouts  2.69 us
    pallas_call x1, Pallas kernels, body(): call(sums_kernel, [SMEM] * 3 + [VMEM] * 4, (jax.ShapeDtypeStruct((near, b...  1.52 us
  transfers between devices with their start and end apart: 1, of which 0 were waited for; matrix products, arithmetic and copies ran while one was open for 0% of the time, Pallas kernels for 0%

profile of v10, /device:TPU:24, one launch (start us, length us, event | category | flops | bytes accessed | tf_op | source)
XLA Modules:
  0.0 74.7 jit_solution(7709558691149945469)
XLA Ops:
  0.0 0.0 copy-start.3
  0.0 0.7 bitcast_add_fusion.patch_ref
  0.7 0.0 copy-done.3
  0.7 0.0 copy-start
  0.7 1.2 %copy-done = bf16[1,32,128,128]{3,2,1,0:T(8,128)(2,1)S(1)} copy-done((bf16[1,32,128,128]{3,2,1,0:T(8,128)(2,1)S(1)}, bf16[1,32,128,128]{3,2,1,0:T(8,128)(2,1)}, u32[]{:S(2)}) %copy-start) | copy-done | bytes 1048600
  1.9 0.0 copy-start.2
  1.9 0.8 %copy-done.2 = f32[3,1,32,128]{3,2,1,0:T(8,128)S(1)} copy-done((f32[3,1,32,128]{3,2,1,0:T(8,128)S(1)}, f32[3,1,32,128]{3,2,1,0:T(8,128)}, u32[]{:S(2)}) %copy-start.2) | copy-done | bytes 49176
  2.7 0.0 copy-start.1
  2.7 0.6 shard_map.82
  3.4 41.2 %all-gather = bf16[1792,128]{1,0:T(8,128)(2,1)S(1)} all-gather(bf16[112,128]{1,0:T(8,128)(2,1)S(1)} %shard_map.82), channel_id=2, replica_groups={{0,1,8,9,16,17,24,25,32,33,40,41,48,49,56,57},{2,3,10,11,18,19,26,27,34..., dimensions={0}, use_global_device_ids=true | all-gather | bytes 487424 | tf_op jit(solution)/shard_map/all_gather | solution.py:189
  44.6 4.8 %collective-permute-start = (bf16[16,112,128]{2,1,0:T(8,128)(2,1)S(1)}, bf16[16,112,128]{2,1,0:T(8,128)(2,1)S(1)}, u32[]{:S(2)}, u32[]{:S(2)}) collective-permute-start(bf16[16,112,128]{2,1,0:T(8,128)(2,1)S(1)} %bitcast.10), channel_id=1, source_target_pairs={{1,65},{3,67},{5,69},{7,71},{9,73},{11,75},{13,77},{15,79},{17,81}... | collective-permute-start | bytes 1376264 | tf_op jit(solution)/shard_map/ppermute | solution.py:197
  49.5 0.1 fusion
  49.6 0.0 copy-start.4
  49.6 11.2 %all-gather.1 = s32[4,2,32]{2,1,0:T(2,128)S(1)} all-gather(s32[1,2,32]{2,1,0:T(2,128)S(1)} %add_bitcast_fusion), channel_id=1, replica_groups={{0,2,4,6},{1,3,5,7},{8,10,12,14},{9,11,13,15},{16,18,20,22},{17,19,21,2..., dimensions={0}, use_global_device_ids=true | all-gather | bytes 1280 | tf_op jit(solution)/shard_map/all_gather | solution.py:208
  60.7 0.0 copy-start.5
  60.7 0.0 copy-start.6
  60.7 0.0 collective-permute-done.row_ref
  60.7 0.0 copy-done.1
  60.8 0.0 copy-done.4
  60.8 0.6 copy-done.5
  61.4 0.0 copy-done.6
  61.4 1.5 %shard_map.83 = (bf16[8,32,384]{2,1,0:T(8,128)(2,1)S(1)}, bf16[32,128,128]{2,1,0:T(8,128)(2,1)S(1)}) custom-call(s32[4]{0:T(128)S(1)} %copy-done.5, f32[3,4]{1,0:T(4,128)S(1)} %copy-done.4, f32[3]{0:T(128)S(1)} %copy-done.6, s32[8,32]{1,0:T(8,128)S(1)} %bitcast.13, bf16[16,112,128]{2,1,0:T(8,128)(2,1)S(1)} %bitcast.12, ...), custom_call_target="tpu_custom_call" | custom-call | flops 352321536 | bytes 2097152 | tf_op jit(solution)/shard_map/pallas_call | solution.py:210
  62.9 10.7 %all_to_all.5.parts_ref = bf16[8,32,384]{2,1,0:T(8,128)(2,1)S(1)} all-to-all(bf16[8,32,384]{2,1,0:T(8,128)(2,1)S(1)} %get-tuple-element.7), channel_id=1, replica_groups={{0,1,2,3,4,5,6,7},{8,9,10,11,12,13,14,15},{16,17,18,19,20,21,22,23},{24..., dimensions={0} | all-to-all | bytes 393216 | tf_op jit(solution)/shard_map/all_to_all | solution.py:219
  73.7 1.0 %shard_map.84 = f32[3,1,32,128]{3,2,1,0:T(8,128)} custom-call(bf16[8,32,384]{2,1,0:T(8,128)(2,1)S(1)} %all_to_all.5.parts_ref, bf16[32,128,128]{2,1,0:T(8,128)(2,1)S(1)} %get-tuple-element.8.turned_ref, s32[1,32]{1,0:T(1,128)S(1)} %copy-done.3), custom_call_target="tpu_custom_call" | custom-call | flops 3145728 | bytes 2097152 | tf_op jit(solution)/shard_map/pallas_call | solution.py:220
  (2 shorter events, 0.0 us)
Async XLA Ops:
  0.0 0.7 copy-start.3
  0.7 1.2 %copy-start = (bf16[1,32,128,128]{3,2,1,0:T(8,128)(2,1)S(1)}, bf16[1,32,128,128]{3,2,1,0:T(8,128)(2,1)}, u32[]{:S(2)}) copy-start(bf16[1,32,128,128]{3,2,1,0:T(8,128)(2,1)} %basis_ref.1) | copy-start | bytes 3145732
  1.9 0.8 %copy-start.2 = (f32[3,1,32,128]{3,2,1,0:T(8,128)S(1)}, f32[3,1,32,128]{3,2,1,0:T(8,128)}, u32[]{:S(2)}) copy-start(f32[3,1,32,128]{3,2,1,0:T(8,128)} %gradient_hbm.1) | copy-start | bytes 147460
  2.7 58.0 %copy-start.1 = (bf16[1,32,128,128]{3,2,1,0:T(8,128)(2,1)S(1)}, bf16[1,32,128,128]{3,2,1,0:T(8,128)(2,1)}, u32[]{:S(2)}) copy-start(bf16[1,32,128,128]{3,2,1,0:T(8,128)(2,1)} %basis_ref.1) | copy-start | bytes 3145732
  44.6 16.2 %collective-permute-start = (bf16[16,112,128]{2,1,0:T(8,128)(2,1)S(1)}, bf16[16,112,128]{2,1,0:T(8,128)(2,1)S(1)}, u32[]{:S(2)}, u32[]{:S(2)}) collective-permute-start(bf16[16,112,128]{2,1,0:T(8,128)(2,1)S(1)} %bitcast.10), channel_id=1, source_target_pairs={{1,65},{3,67},{5,69},{7,71},{9,73},{11,75},{13,77},{15,79},{17,81}... | collective-permute-start | bytes 1376264 | tf_op jit(solution)/shard_map/ppermute | solution.py:197
  49.6 11.2 %copy-start.4 = (f32[3,4]{1,0:T(4,128)S(1)}, f32[3,4]{1,0:T(4,128)}, u32[]{:S(2)}) copy-start(f32[3,4]{1,0:T(4,128)} %band_ref.1) | copy-start | bytes 148
  60.7 0.7 copy-start.5
  60.7 0.7 copy-start.6
